TPU v7x, 256 devices: a whole 4x4x8 slice. The times are simulated.
256 devices in a mesh: ctx: 32 (over x, z_hi, core), head: 8 (over y, z_lo).
Axes of the slice: x: 4, y: 4, z: 8 (z_hi: 4, z_lo: 2; z = z_hi * 2 + z_lo), core: 2. Of those that a mesh axis runs over, the one named last changes fastest.
Arguments:
- keys: bfloat16 [16384, 4096], P('ctx', 'head'), may hold values from -6 to 6
- values: bfloat16 [16384, 4096], P('ctx', 'head'), may hold values from -6 to 6
- rates: float32 [8, 16384], P('head', 'ctx'), may hold values from 0.05 to 1
- queries: bfloat16 [16384, 4096], P(('ctx', 'head')), may hold values from -6 to 6
- fast_weights: bfloat16 [8, 3, 512, 512], P('head'), may hold values from -4 to 4
- gate: bfloat16 [16384, 4096], P(('ctx', 'head')), may hold values from -6 to 6
- gain: float32 [4096], replicated, may hold values from 0.1 to 1.9
Outputs:
- layer_out: bfloat16 [16384, 4096], P(('ctx', 'head'))
- new_weights: bfloat16 [8, 3, 512, 512], P('head')
All inputs are finite; a program needn't handle non-finite values.
Results may differ from a plain program's by a relative error of at most 0.023.
Values may be sent and summed in bfloat16 or wider, within the bound.
A program may use at most 64 MiB of HBM per device.

v0:
```python
import jax
import jax.numpy as jnp
from jax import lax
from jax.sharding import PartitionSpec as P

NS_STEPS = 5


coef_a = 3.4445
coef_b = -4.775
coef_c = 2.0315


def bmm(form, left, right):
    return jnp.einsum(form, left, right, preferred_element_type=jnp.float32)


def memory_read(query_rows, weight_set):
    scale = weight_set.shape[-1] ** (-0.5)
    r_one = bmm("thi,hij->thj", query_rows, weight_set[:, 0]) * scale
    r_three = bmm("thi,hij->thj", query_rows, weight_set[:, 1]) * scale
    hq = (jax.nn.silu(r_one) * r_three).astype(jnp.bfloat16)
    return (bmm("thj,hjc->thc", hq, weight_set[:, 2]) * scale).astype(jnp.bfloat16)


def poly_step(iterate_part, gram_part, square_part, whole):
    poly = (coef_b * gram_part.astype(jnp.float32) + coef_c * square_part).astype(jnp.bfloat16)
    return (coef_a * iterate_part.astype(jnp.float32) + bmm("hmrk,hmkc->hmrc", poly, whole)).astype(
        jnp.bfloat16
    )


def local(keys, values, rates, queries, fast_weights, gate, gain):
    heads_here = fast_weights.shape[0]
    width = fast_weights.shape[-1]
    scale = width ** (-0.5)
    step_size = 0.4 * jnp.sqrt(jnp.float32(width))
    tok_rows = keys.shape[0]
    key_rows = keys.reshape(tok_rows, heads_here, width)
    value_rows = values.reshape(tok_rows, heads_here, width)
    g_one = bmm("thi,hij->thj", key_rows, fast_weights[:, 0]) * scale
    g_three = bmm("thi,hij->thj", key_rows, fast_weights[:, 1]) * scale
    sig = jax.nn.sigmoid(g_one)
    hidden = (g_one * sig * g_three).astype(jnp.bfloat16)
    grad_out = (-(rates.T[:, :, None] * value_rows.astype(jnp.float32))).astype(jnp.bfloat16)
    d_two = bmm("thj,thc->hjc", hidden, grad_out) * scale
    d_hidden = bmm("thc,hjc->thj", grad_out, fast_weights[:, 2]) * scale
    dg_one = (d_hidden * g_three * sig * (1.0 + g_one * (1.0 - sig))).astype(jnp.bfloat16)
    dg_three = (d_hidden * (g_one * sig)).astype(jnp.bfloat16)
    d_one = bmm("thi,thj->hij", key_rows, dg_one) * scale
    d_three = bmm("thi,thj->hij", key_rows, dg_three) * scale
    partial_value = jnp.stack([d_one, d_three, d_two], axis=1)
    grads = lax.psum(partial_value.astype(jnp.bfloat16), "ctx").astype(jnp.float32)
    total = jnp.sum(grads * grads, axis=(2, 3), keepdims=True)
    iterate = (grads / (jnp.sqrt(total) + 1e-07)).astype(jnp.bfloat16)
    for step in range(NS_STEPS):
        gram = bmm("hmrc,hmkc->hmrk", iterate, iterate).astype(jnp.bfloat16)
        square = bmm("hmrk,hmkc->hmrc", gram, gram)
        iterate = poly_step(iterate, gram, square, iterate)
    new_weights = (
        fast_weights.astype(jnp.float32) - step_size * iterate.astype(jnp.float32)
    ).astype(jnp.bfloat16)
    query_rows = queries.shape[0]
    all_heads = queries.shape[1] // width
    query_heads = queries.reshape(query_rows, all_heads, width)
    owned = lax.all_to_all(query_heads, "head", split_axis=1, concat_axis=0, tiled=True)
    read_owned = memory_read(owned, fast_weights)
    read = lax.all_to_all(read_owned, "head", split_axis=0, concat_axis=1, tiled=True)
    read32 = read.astype(jnp.float32)
    mean_sq = jnp.mean(read32 * read32, axis=-1, keepdims=True)
    gate32 = gate.astype(jnp.float32).reshape(query_rows, all_heads, width)
    normed = (
        read32 * lax.rsqrt(mean_sq + 1e-06) * gain.reshape(all_heads, width) * jax.nn.silu(gate32)
    )
    return (normed.reshape(query_rows, all_heads * width).astype(jnp.bfloat16), new_weights)


def solution(mesh):
    in_specs = (
        P("ctx", "head"),
        P("ctx", "head"),
        P("head", "ctx"),
        P(("ctx", "head"), None),
        P("head", None, None, None),
        P(("ctx", "head"), None),
        P(),
    )
    out_specs = (P(("ctx", "head"), None), P("head", None, None, None))
    return jax.shard_map(local, mesh=mesh, in_specs=in_specs, out_specs=out_specs, check_vma=False)
```

profile of v0, /device:TPU:1, one launch (start us, length us, event | category | flops | bytes accessed | tf_op | source)
XLA Modules:
  0.0 371.1 jit_solution(18282563990789065375)
XLA Ops:
  7.2 0.0 copy-start
  7.2 0.0 copy-start.2
  7.2 0.0 all-reduce.2.cloned.1.call-start
  7.2 1.0 copy-done
  8.2 1.5 fusion.17
  9.7 0.0 copy-done.2
  9.8 0.0 copy-start.7
  9.8 0.0 copy-start.8
  9.8 0.5 fusion.18
  10.3 0.5 copy-done.7
  10.8 0.0 copy-done.8
  10.8 0.6 fusion.19
  11.4 0.6 fusion.30
  12.0 0.8 fusion.32
  12.8 0.6 fusion.31
  13.4 1.3 pad_maximum_fusion
  14.7 0.0 copy-start.4
  14.7 0.0 all-reduce.2.cloned.1.call-update
  14.7 1.0 copy-done.4
  15.8 15.4 %all_to_all.24 = bf16[64,8,512]{2,0,1:T(8,128)(2,1)S(1)} all-to-all(bf16[64,8,512]{2,0,1:T(8,128)(2,1)S(1)} %bitcast.165), channel_id=1, replica_groups=mesh['ctx'=32,'head'=8] {'head'}, dimensions={1} | all-to-all | bytes 1048576 | tf_op jit(solution)/shard_map/all_to_all | solution.py:66
  31.2 1.5 fusion.22
  32.7 2.1 fusion.33
  34.8 0.5 broadcast.145
  35.3 1.0 reduce.4
  36.3 1.2 reshape.303
  37.5 3.7 all-to-all-start.1
  41.2 265.5 %all-reduce.2.cloned.1.call-done = bf16[1,3,512,512]{3,2,1,0:T(8,128)(2,1)} async-done(((bf16[1,3,512,512]{3,2,1,0:T(8,128)(2,1)}), bf16[1,3,512,512]{3,2,1,0:T(8,128)(2,1)}) %all-reduce.2.cloned.1.call-update) | async-done | bytes 1572880 | tf_op jit(solution)/shard_map/psum | solution.py:53
  306.7 0.0 copy-start.1
  306.7 2.0 fusion
  308.7 0.0 copy-done.1
  308.7 2.3 convolution_convert_fusion.4
  311.0 5.8 %fusion.6 = bf16[1,3,512,512]{3,2,1,0:T(8,128)(2,1)} fusion(bf16[3,512,512]{2,1,0:T(8,128)(2,1)} %convolution_convert_fusion.4, f32[3]{0:T(128)S(1)} %sqrt_add_fusion, bf16[1,3,512,512]{3,2,1,0:T(8,128)(2,1)S(1)} %copy-done.1), kind=kOutput, calls=%fused_computation.13 | convolution fusion | flops 1622409216 | bytes 4718604 | tf_op jit(solution)/shard_map/hmrk,hmkc->hmrc/dot_general | solution.py:15
  316.8 0.0 copy-start.9
  316.8 4.2 %convolution_convert_fusion.3 = bf16[3,512,512]{2,1,0:T(8,128)(2,1)} fusion(bf16[1,3,512,512]{3,2,1,0:T(8,128)(2,1)} %fusion.6), kind=kOutput, calls=%fused_computation.23 | convolution fusion | flops 806092800 | bytes 3145728 | tf_op jit(solution)/shard_map/hmrc,hmkc->hmrk/dot_general | solution.py:15
  320.9 0.0 copy-done.9
  321.0 5.7 %fusion.5 = bf16[1,3,512,512]{3,2,1,0:T(8,128)(2,1)} fusion(bf16[1,3,512,512]{3,2,1,0:T(8,128)(2,1)S(1)} %copy-done.9, bf16[3,512,512]{2,1,0:T(8,128)(2,1)} %convolution_convert_fusion.3), kind=kOutput, calls=%fused_computation.11 | convolution fusion | flops 1617690624 | bytes 4718592 | tf_op jit(solution)/shard_map/hmrk,hmkc->hmrc/dot_general | solution.py:15
  326.7 0.0 copy-start.10
  326.7 4.2 %convolution_convert_fusion.2 = bf16[3,512,512]{2,1,0:T(8,128)(2,1)} fusion(bf16[1,3,512,512]{3,2,1,0:T(8,128)(2,1)} %fusion.5), kind=kOutput, calls=%fused_computation.22 | convolution fusion | flops 806092800 | bytes 3145728 | tf_op jit(solution)/shard_map/hmrc,hmkc->hmrk/dot_general | solution.py:15
  330.9 0.0 copy-done.10
  330.9 5.7 %fusion.4 = bf16[1,3,512,512]{3,2,1,0:T(8,128)(2,1)} fusion(bf16[1,3,512,512]{3,2,1,0:T(8,128)(2,1)S(1)} %copy-done.10, bf16[3,512,512]{2,1,0:T(8,128)(2,1)} %convolution_convert_fusion.2), kind=kOutput, calls=%fused_computation.9 | convolution fusion | flops 1617690624 | bytes 4718592 | tf_op jit(solution)/shard_map/hmrk,hmkc->hmrc/dot_general | solution.py:15
  336.6 0.0 copy-start.11
  336.6 4.2 %convolution_convert_fusion.1 = bf16[3,512,512]{2,1,0:T(8,128)(2,1)} fusion(bf16[1,3,512,512]{3,2,1,0:T(8,128)(2,1)} %fusion.4), kind=kOutput, calls=%fused_computation.21 | convolution fusion | flops 806092800 | bytes 3145728 | tf_op jit(solution)/shard_map/hmrc,hmkc->hmrk/dot_general | solution.py:15
  340.8 0.0 copy-done.11
  340.8 5.7 %fusion.3 = bf16[1,3,512,512]{3,2,1,0:T(8,128)(2,1)} fusion(bf16[1,3,512,512]{3,2,1,0:T(8,128)(2,1)S(1)} %copy-done.11, bf16[3,512,512]{2,1,0:T(8,128)(2,1)} %convolution_convert_fusion.1), kind=kOutput, calls=%fused_computation.7 | convolution fusion | flops 1617690624 | bytes 4718592 | tf_op jit(solution)/shard_map/hmrk,hmkc->hmrc/dot_general | solution.py:15
  346.5 0.0 copy-start.3
  346.5 4.2 %convolution_convert_fusion = bf16[3,512,512]{2,1,0:T(8,128)(2,1)} fusion(bf16[1,3,512,512]{3,2,1,0:T(8,128)(2,1)} %fusion.3), kind=kOutput, calls=%fused_computation.20 | convolution fusion | flops 806092800 | bytes 3145728 | tf_op jit(solution)/shard_map/hmrc,hmkc->hmrk/dot_general | solution.py:15
  350.7 0.0 copy-done.3
  350.7 6.6 %subtract_convert_fusion = bf16[1,3,512,512]{3,2,1,0:T(8,128)(2,1)} fusion(bf16[1,3,512,512]{3,2,1,0:T(8,128)(2,1)S(1)} %copy-done.3, bf16[1,3,512,512]{3,2,1,0:T(8,128)(2,1)} %fusion.3, bf16[3,512,512]{2,1,0:T(8,128)(2,1)} %convolution_convert_fusion), kind=kOutput, calls=%fused_computation.14 | convolution fusion | flops 1621622784 | bytes 6291456 | tf_op jit(solution)/shard_map/hmrk,hmkc->hmrc/dot_general | solution.py:15
  357.3 0.0 all-to-all-done.1
  357.3 0.5 reshape.304
  357.9 1.1 convert_element_type.219
  358.9 1.7 multiply_reduce_fusion
  360.6 0.6 copy.35
  361.2 0.6 copy.47
  361.9 0.1 reshape.301
  362.0 0.1 copy.36
  362.0 0.0 copy-start.5
  362.0 0.0 copy-start.6
  362.0 0.1 mul.221
  362.2 0.6 copy.48
  362.8 0.3 copy-done.5
  363.1 0.0 copy-done.6
  363.1 1.1 fusion.40
  (3 shorter events, 0.1 us)
Async XLA Ops:
  7.2 1.0 copy-start
  7.2 2.6 copy-start.2
  7.2 299.5 %all-reduce.2.cloned.1.call-start = ((), (), s32[]{:S(2)}) async-start(), calls=%async_computation.2 | async-start | bytes 3145728 | tf_op jit(solution)/shard_map/psum | solution.py:53
  9.8 1.0 copy-start.7
  9.8 1.0 copy-start.8
  14.7 1.0 copy-start.4
  37.5 319.8 %all-to-all-start.1 = ((bf16[8,2,16384]{2,1,0:T(2,128)(2,1)}), bf16[8,2,16384]{2,1,0:T(2,128)(2,1)S(1)}, u32[]{:S(2)}, u32[]{:S(2)}) async-start(bf16[8,2,16384]{2,1,0:T(2,128)(2,1)} %reshape.303), calls=%async_computation.1 | async-start | bytes 1048576 | tf_op jit(solution)/shard_map/all_to_all | solution.py:68
  306.7 2.0 copy-start.1
  316.8 4.2 %copy-start.9 = (bf16[1,3,512,512]{3,2,1,0:T(8,128)(2,1)S(1)}, bf16[1,3,512,512]{3,2,1,0:T(8,128)(2,1)}, u32[]{:S(2)}) copy-start(bf16[1,3,512,512]{3,2,1,0:T(8,128)(2,1)} %fusion.6) | copy-start | bytes 4718596
  326.7 4.2 %copy-start.10 = (bf16[1,3,512,512]{3,2,1,0:T(8,128)(2,1)S(1)}, bf16[1,3,512,512]{3,2,1,0:T(8,128)(2,1)}, u32[]{:S(2)}) copy-start(bf16[1,3,512,512]{3,2,1,0:T(8,128)(2,1)} %fusion.5) | copy-start | bytes 4718596
  336.6 4.2 %copy-start.11 = (bf16[1,3,512,512]{3,2,1,0:T(8,128)(2,1)S(1)}, bf16[1,3,512,512]{3,2,1,0:T(8,128)(2,1)}, u32[]{:S(2)}) copy-start(bf16[1,3,512,512]{3,2,1,0:T(8,128)(2,1)} %fusion.4) | copy-start | bytes 4718596
  346.5 4.2 %copy-start.3 = (bf16[1,3,512,512]{3,2,1,0:T(8,128)(2,1)S(1)}, bf16[1,3,512,512]{3,2,1,0:T(8,128)(2,1)}, u32[]{:S(2)}) copy-start(bf16[1,3,512,512]{3,2,1,0:T(8,128)(2,1)} %param.11) | copy-start | bytes 4718596
  362.0 1.0 copy-start.5
  362.0 1.0 copy-start.6
Sparse Core Ops, SparseCore 0:
  14.9 291.7 all-reduce.1
where the time goes:
time: 371 us
  waiting for transfers between devices  266 us (72%)
  matrix products  56.7 us (15%)
  blocking collectives  15.4 us (4%)
  between operations  14.2 us (4%)
  other arithmetic  8.28 us (2%)
  local copies, waits for them, and re-layouts  7.21 us (2%)
  starting transfers between devices  3.71 us (1%)
    psum x1, waiting for transfers between devices, local(): lax.psum(partial_value.astype(jnp.bfloat16), 'ctx').astype(jnp.float32)  266 us
    dot_general x18, matrix products, bmm(): return jnp.einsum(form, left, right, preferred_element_type=jnp.float32)  56.7 us
    all_to_all x1, blocking collectives, local(): lax.all_to_all(query_heads, 'head', split_axis=1, concat_axis=0, tiled=True)  15.4 us
  transfers between devices with their start and end apart: 2, of which 1 were waited for; matrix products, arithmetic and copies ran while one was open for 15% of the time, Pallas kernels for 0%

commit v1 on v0

v1 whole, which is shorter than its diff:
```python
import functools

import jax
import jax.numpy as jnp
from jax import lax
from jax.experimental import pallas as pl
from jax.experimental.pallas import tpu as pltpu
from jax.sharding import PartitionSpec as P

NS_STEPS = 5
DH = 512
HEADS = 8
SCALE = DH ** (-0.5)
COEF_A, COEF_B, COEF_C = 3.4445, -4.775, 2.0315
F32, BF16 = jnp.float32, jnp.bfloat16
NT = (((1,), (1,)), ((), ()))
TN = (((0,), (0,)), ((), ()))
NN = (((1,), (0,)), ((), ()))


def mat(left, right, dims=NN):
    return lax.dot_general(left, right, dims, preferred_element_type=F32)


def memory_kernel(
    keys, values, rates, queries, weights, gate, gain,
    layer_out, new_weights,
    k_v, v_v, w_v, gate_v, q_buf, r_out, r_in, out_v, nw_v,
    loc, c_recv, part, x_recv, z_buf, full, x_it, gram, dg_v,
    in_sem, out_sem, q_ss, q_rs, r_ss, r_rs, c_ss, c_rs, x_ss, x_rs, z_ss, z_rs, a_ss, a_rs, f_ss, f_rs,
):
    ctx, head = lax.axis_index("ctx"), lax.axis_index("head")
    xi, zi, core = ctx // 8, (ctx // 2) % 4, ctx % 2

    def at(x, z, c):
        return (x * 8 + z * 2 + c, head)

    def x_other(d):
        return (xi + d) % 4

    def z_other(d):
        return (zi + d) % 4

    sibling = at(xi, zi, 1 - core)
    heads_other = [(head + d) % HEADS for d in range(1, HEADS)]

    def remote(src, dst, ss, rs, target):
        return pltpu.make_async_remote_copy(
            src_ref=src, dst_ref=dst, send_sem=ss, recv_sem=rs,
            device_id=target, device_id_type=pl.DeviceIdType.MESH,
        )

    barrier = pltpu.get_barrier_semaphore()
    partners = [sibling] + [at(x_other(d), zi, core) for d in (1, 2, 3)]
    partners += [at(xi, z_other(d), core) for d in (1, 2, 3)] + [(ctx, h) for h in heads_other]
    for partner in partners:
        pl.semaphore_signal(barrier, inc=1, device_id=partner, device_id_type=pl.DeviceIdType.MESH)

    loads = [
        pltpu.make_async_copy(keys, k_v, in_sem.at[0]),
        pltpu.make_async_copy(weights.at[0, 0], w_v.at[0], in_sem.at[1]),
        pltpu.make_async_copy(weights.at[0, 1], w_v.at[1], in_sem.at[2]),
        pltpu.make_async_copy(values, v_v, in_sem.at[3]),
        pltpu.make_async_copy(weights.at[0, 2], w_v.at[2], in_sem.at[4]),
        pltpu.make_async_copy(
            queries.at[:, pl.ds(pl.multiple_of(head * DH, DH), DH)], q_buf.at[head], in_sem.at[5]
        ),
        pltpu.make_async_copy(gate, gate_v, in_sem.at[6]),
    ]
    for load in loads:
        load.start()

    loads[0].wait()
    loads[1].wait()
    g_one = mat(k_v[...], w_v[0]) * SCALE
    loads[2].wait()
    g_three = mat(k_v[...], w_v[1]) * SCALE
    sig = jax.nn.sigmoid(g_one)
    hidden = (g_one * sig * g_three).astype(BF16)
    loads[3].wait()
    rate_col = jnp.broadcast_to(rates[...], (128, DH)).T
    rate_wide = jnp.concatenate([rate_col] * 4, axis=1)
    grad_out = (-(rate_wide * v_v[...].astype(F32))).astype(BF16)
    loc[2] = (mat(hidden, grad_out, TN) * SCALE).astype(BF16)

    core_copies, x_copies, z_copies, a_copies, f_copies = {}, {}, {}, {}, {}

    def core_send(m):
        core_copies[m] = remote(
            loc.at[m, pl.ds(pl.multiple_of((1 - core) * 256, 256), 256)], c_recv.at[m],
            c_ss.at[m], c_rs.at[m], sibling,
        )
        core_copies[m].start()

    def x_send(m):
        core_copies[m].wait_recv()
        mine = loc[m, pl.ds(pl.multiple_of(core * 256, 256), 256), :].astype(F32)
        part[m] = (mine + c_recv[m].astype(F32)).astype(BF16).reshape(4, 64, DH)
        x_copies[m] = []
        for d in (1, 3, 2):
            copy = remote(
                part.at[m, x_other(d)], x_recv.at[m, d - 1], x_ss.at[m, d - 1], x_rs.at[m, d - 1],
                at(x_other(d), zi, core),
            )
            copy.start()
            x_copies[m].append(copy)

    def z_send(m):
        for copy in x_copies[m]:
            copy.wait_recv()
        total = part[m, xi].astype(F32)
        for d in range(3):
            total = total + x_recv[m, d].astype(F32)
        z_buf[m, zi] = total.astype(BF16)
        z_copies[m] = []
        for d in (1, 3, 2):
            copy = remote(
                z_buf.at[m, zi], z_buf.at[m, zi], z_ss.at[m, d - 1], z_rs.at[m, d - 1],
                at(xi, z_other(d), core),
            )
            copy.start()
            z_copies[m].append(copy)

    def forward(m, which, chunk):
        copy = remote(
            full.at[m, core, chunk], full.at[m, core, chunk], f_ss.at[m, which], f_rs.at[m, which], sibling
        )
        copy.start()
        f_copies[m].append(copy)

    def a_send(m):
        for copy in z_copies[m]:
            copy.wait_recv()
        total = z_buf[m, 0].astype(F32)
        for z in range(1, 4):
            total = total + z_buf[m, z].astype(F32)
        full[m, core, xi] = total.astype(BF16)
        a_copies[m] = []
        for d in (1, 3, 2):
            copy = remote(
                full.at[m, core, xi], full.at[m, core, xi], a_ss.at[m, d - 1], a_rs.at[m, d - 1],
                at(x_other(d), zi, core),
            )
            copy.start()
            a_copies[m].append(copy)
        f_copies[m] = []
        forward(m, 0, xi)

    def f_send(m):
        for i, d in enumerate((1, 3, 2)):
            a_copies[m][i].wait_recv()
            forward(m, d, (xi + 4 - d) % 4)

    def gather_end(m):
        for copy in f_copies[m]:
            copy.wait_recv()

    pl.semaphore_wait(barrier, len(partners))
    core_send(2)

    q_copies = []
    for d, h in enumerate(heads_other):
        copy = remote(
            queries.at[:, pl.ds(pl.multiple_of(h * DH, DH), DH)], q_buf.at[head], q_ss.at[d], q_rs.at[d], (ctx, h)
        )
        copy.start()
        q_copies.append(copy)

    loads[4].wait()
    d_hidden = mat(grad_out, w_v[2], NT) * SCALE
    dg_v[0] = (d_hidden * g_three * sig * (1.0 + g_one * (1.0 - sig))).astype(BF16)
    dg_v[1] = (d_hidden * (g_one * sig)).astype(BF16)
    x_send(2)
    loc[0] = (mat(k_v[...], dg_v[0], TN) * SCALE).astype(BF16)
    core_send(0)
    loc[1] = (mat(k_v[...], dg_v[1], TN) * SCALE).astype(BF16)
    core_send(1)
    x_send(0)
    x_send(1)
    z_send(2)

    loads[5].wait()
    for copy in q_copies:
        copy.wait_recv()
    q_rows = q_buf[...].reshape(HEADS * 64, DH)
    r_one = mat(q_rows, w_v[0]) * SCALE
    r_three = mat(q_rows, w_v[1]) * SCALE
    hq = (r_one * jax.nn.sigmoid(r_one) * r_three).astype(BF16)
    r_out[...] = (mat(hq, w_v[2]) * SCALE).astype(BF16).reshape(HEADS, 64, DH)
    z_send(0)
    z_send(1)
    r_copies = []
    for d, h in enumerate(heads_other):
        copy = remote(r_out.at[h], r_in.at[head], r_ss.at[d], r_rs.at[d], (ctx, h))
        copy.start()
        r_copies.append(copy)
    r_in[head] = r_out[head]

    a_send(2)
    a_send(0)
    a_send(1)

    loads[6].wait()
    for copy in r_copies:
        copy.wait_recv()
    for h in range(HEADS):
        cols = slice(h * DH, (h + 1) * DH)
        read = r_in[h].astype(F32)
        mean_sq = jnp.mean(read * read, axis=-1, keepdims=True)
        gated = gate_v[:, cols].astype(F32)
        out_v[:, cols] = (
            read * lax.rsqrt(mean_sq + 1e-06) * gain[:, cols] * (gated * jax.nn.sigmoid(gated))
        ).astype(BF16)
    stores = [pltpu.make_async_copy(out_v, layer_out, out_sem.at[3])]
    stores[0].start()

    def orthogonalise(m):
        grad = full[m].reshape(DH, DH).astype(F32)
        norm = jnp.sqrt(jnp.sum(grad * grad)) + 1e-07
        x_it[m] = (grad / norm).astype(BF16)

        def step(_, carry):
            gram[m] = mat(x_it[m], x_it[m], NT).astype(BF16)
            square = mat(gram[m], gram[m])
            poly = (COEF_B * gram[m].astype(F32) + COEF_C * square).astype(BF16)
            x_it[m] = (COEF_A * x_it[m].astype(F32) + mat(poly, x_it[m])).astype(BF16)
            return carry

        lax.fori_loop(0, NS_STEPS, step, 0)
        step_size = 0.4 * DH ** 0.5
        nw_v[m] = (w_v[m].astype(F32) - step_size * x_it[m].astype(F32)).astype(BF16)
        store = pltpu.make_async_copy(nw_v.at[m], new_weights.at[0, m], out_sem.at[m])
        store.start()
        stores.append(store)

    f_send(2)
    gather_end(2)
    orthogonalise(2)
    f_send(0)
    gather_end(0)
    orthogonalise(0)
    f_send(1)
    gather_end(1)
    orthogonalise(1)

    for group in (x_copies, z_copies, a_copies, f_copies):
        for m in range(3):
            for copy in group[m]:
                copy.wait_send()
    for m in range(3):
        core_copies[m].wait_send()
    for copy in q_copies + r_copies:
        copy.wait_send()
    for store in stores:
        store.wait()


def local(keys, values, rates, queries, fast_weights, gate, gain):
    anywhere = pl.BlockSpec(memory_space=pl.ANY)
    vmem = pl.BlockSpec(memory_space=pltpu.VMEM)
    dma = pltpu.SemaphoreType.DMA
    return pl.pallas_call(
        memory_kernel,
        name="memory_layer",
        out_shape=(
            jax.ShapeDtypeStruct((64, HEADS * DH), BF16),
            jax.ShapeDtypeStruct((1, 3, DH, DH), BF16),
        ),
        in_specs=[anywhere, anywhere, vmem, anywhere, anywhere, anywhere, vmem],
        out_specs=(anywhere, anywhere),
        scratch_shapes=[
            pltpu.VMEM((512, DH), BF16),
            pltpu.VMEM((512, DH), BF16),
            pltpu.VMEM((3, DH, DH), BF16),
            pltpu.VMEM((64, HEADS * DH), BF16),
            pltpu.VMEM((HEADS, 64, DH), BF16),
            pltpu.VMEM((HEADS, 64, DH), BF16),
            pltpu.VMEM((HEADS, 64, DH), BF16),
            pltpu.VMEM((64, HEADS * DH), BF16),
            pltpu.VMEM((3, DH, DH), BF16),
            pltpu.VMEM((3, DH, DH), BF16),
            pltpu.VMEM((3, 256, DH), BF16),
            pltpu.VMEM((3, 4, 64, DH), BF16),
            pltpu.VMEM((3, 3, 64, DH), BF16),
            pltpu.VMEM((3, 4, 64, DH), BF16),
            pltpu.VMEM((3, 2, 4, 64, DH), BF16),
            pltpu.VMEM((3, DH, DH), BF16),
            pltpu.VMEM((3, DH, DH), BF16),
            pltpu.VMEM((2, DH, DH), BF16),
            dma((7,)), dma((4,)),
            dma((7,)), dma((7,)), dma((7,)), dma((7,)),
            dma((3,)), dma((3,)),
            dma((3, 3)), dma((3, 3)), dma((3, 3)), dma((3, 3)), dma((3, 3)), dma((3, 3)),
            dma((3, 4)), dma((3, 4)),
        ],
        compiler_params=pltpu.CompilerParams(
            collective_id=0, has_side_effects=True, vmem_limit_bytes=48 * 2**20
        ),
    )(keys, values, rates, queries, fast_weights, gate, gain.reshape(1, HEADS * DH))


def solution(mesh):
    in_specs = (
        P("ctx", "head"),
        P("ctx", "head"),
        P("head", "ctx"),
        P(("ctx", "head"), None),
        P("head", None, None, None),
        P(("ctx", "head"), None),
        P(),
    )
    out_specs = (P(("ctx", "head"), None), P("head", None, None, None))
    return jax.shard_map(local, mesh=mesh, in_specs=in_specs, out_specs=out_specs, check_vma=False)
```

time: 371 us -> 75.9 us (0.20)
  waiting for transfers between devices: 266 us -> 0 us
  Pallas kernels: 0 us -> 66 us
  matrix products: 56.7 us -> 0 us
  blocking collectives: 15.4 us -> 0 us
  between operations: 14.2 us -> 0.66 us
  other arithmetic: 8.28 us -> 0 us
  starting transfers between devices: 3.71 us -> 0 us
    psum x1 -> x0, waiting for transfers between devices: 266 us -> none  [local(): lax.psum(partial_value.astype(jnp.bfloat16), 'ctx').astype(jnp.float32)]
    pallas_call x0 -> x1, Pallas kernels: none -> 66 us  [local(): pl.pallas_call(memory_kernel, name='memory_layer', out_shape=(jax.ShapeDt...]
    dot_general x18 -> x0, matrix products: 56.7 us -> none  [bmm(): return jnp.einsum(form, left, right, preferred_element_type=jnp.float32)]
    all_to_all x1 -> x0, blocking collectives: 15.4 us -> none  [local(): lax.all_to_all(query_heads, 'head', split_axis=1, concat_axis=0, tiled=True)]
    unnamed x28 -> x16, local copies, waits for them, and re-layouts: 5.75 us -> 8.9 us
  transfers between devices with their start and end apart: 2 -> 0, of which waited for: 1 -> 0; matrix products, arithmetic and copies ran while one was open for 15% -> 0% of each run, Pallas kernels for 0% -> 0%
where the time goes in v1:
time: 75.9 us; the launch traced here: 75.6 us
  Pallas kernels  66 us (87%)
  local copies, waits for them, and re-layouts  8.9 us (12%)
    pallas_call x1, Pallas kernels, local(): pl.pallas_call(memory_kernel, name='memory_layer', out_shape=(jax.ShapeDt...  66 us
    unnamed x16, local copies, waits for them, and re-layouts  8.9 us

profile of v1, /device:TPU:1, one launch (start us, length us, event | category | flops | bytes accessed | tf_op | source)
XLA Modules:
  0.0 75.6 jit_solution(11189129937383964816)
XLA Ops:
  0.6 0.0 copy-start
  0.6 1.4 %copy-done = bf16[1,3,512,512]{3,2,1,0:T(8,128)(2,1)S(1)} copy-done((bf16[1,3,512,512]{3,2,1,0:T(8,128)(2,1)S(1)}, bf16[1,3,512,512]{3,2,1,0:T(8,128)(2,1)}, u32[]{:S(2)}) %copy-start) | copy-done | bytes 1572888
  2.0 0.0 copy-start.1
  2.0 1.0 %copy-done.1 = bf16[512,512]{1,0:T(8,128)(2,1)S(1)} copy-done((bf16[512,512]{1,0:T(8,128)(2,1)S(1)}, bf16[512,512]{1,0:T(8,128)(2,1)}, u32[]{:S(2)}) %copy-start.1) | copy-done | bytes 524312
  3.1 0.0 copy-start.2
  3.1 1.0 %copy-done.2 = bf16[512,512]{1,0:T(8,128)(2,1)S(1)} copy-done((bf16[512,512]{1,0:T(8,128)(2,1)S(1)}, bf16[512,512]{1,0:T(8,128)(2,1)}, u32[]{:S(2)}) %copy-start.2) | copy-done | bytes 524312
  4.1 0.0 copy-start.3
  4.1 1.0 %copy-done.3 = bf16[64,4096]{1,0:T(8,128)(2,1)S(1)} copy-done((bf16[64,4096]{1,0:T(8,128)(2,1)S(1)}, bf16[64,4096]{1,0:T(8,128)(2,1)}, u32[]{:S(2)}) %copy-start.3) | copy-done | bytes 524312
  5.2 0.0 copy-start.4
  5.2 1.0 %copy-done.4 = bf16[64,4096]{1,0:T(8,128)(2,1)S(1)} copy-done((bf16[64,4096]{1,0:T(8,128)(2,1)S(1)}, bf16[64,4096]{1,0:T(8,128)(2,1)}, u32[]{:S(2)}) %copy-start.4) | copy-done | bytes 524312
  6.2 0.0 copy-start.5
  6.2 0.7 copy-done.5
  6.9 0.0 copy-start.6
  6.9 0.7 copy-done.6
  7.6 66.0 %memory_layer.1 = (bf16[64,4096]{1,0:T(8,128)(2,1)S(1)}, bf16[1,3,512,512]{3,2,1,0:T(8,128)(2,1)S(1)}) custom-call(bf16[512,512]{1,0:T(8,128)(2,1)S(1)} %copy-done.1, bf16[512,512]{1,0:T(8,128)(2,1)S(1)} %copy-done.2, f32[1,512]{1,0:T(1,128)S(1)} %copy-done.6, bf16[64,4096]{1,0:T(8,128)(2,1)S(1)} %copy-done.3, bf16[1,3,512,512]{3,2,1,0:T(8,128)(2,1)S(1)} %copy-done, ...), custom_call_target="tpu_custom_call" | custom-call | tf_op jit(solution)/shard_map/memory_layer/pallas_call | solution.py:262
  73.6 0.8 %copy.11 = bf16[64,4096]{1,0:T(8,128)(2,1)} copy(bf16[64,4096]{1,0:T(8,128)(2,1)S(1)} %get-tuple-element.4) | data formatting | bytes 1048576
  74.4 1.1 %copy.12 = bf16[1,3,512,512]{3,2,1,0:T(8,128)(2,1)} copy(bf16[1,3,512,512]{3,2,1,0:T(8,128)(2,1)S(1)} %get-tuple-element.5) | data formatting | bytes 3145728
Async XLA Ops:
  0.6 1.4 %copy-start = (bf16[1,3,512,512]{3,2,1,0:T(8,128)(2,1)S(1)}, bf16[1,3,512,512]{3,2,1,0:T(8,128)(2,1)}, u32[]{:S(2)}) copy-start(bf16[1,3,512,512]{3,2,1,0:T(8,128)(2,1)} %weights.1) | copy-start | bytes 4718596
  2.0 1.0 %copy-start.1 = (bf16[512,512]{1,0:T(8,128)(2,1)S(1)}, bf16[512,512]{1,0:T(8,128)(2,1)}, u32[]{:S(2)}) copy-start(bf16[512,512]{1,0:T(8,128)(2,1)} %keys.1) | copy-start | bytes 1572868
  3.1 1.0 %copy-start.2 = (bf16[512,512]{1,0:T(8,128)(2,1)S(1)}, bf16[512,512]{1,0:T(8,128)(2,1)}, u32[]{:S(2)}) copy-start(bf16[512,512]{1,0:T(8,128)(2,1)} %values.1) | copy-start | bytes 1572868
  4.1 1.0 %copy-start.3 = (bf16[64,4096]{1,0:T(8,128)(2,1)S(1)}, bf16[64,4096]{1,0:T(8,128)(2,1)}, u32[]{:S(2)}) copy-start(bf16[64,4096]{1,0:T(8,128)(2,1)} %queries.1) | copy-start | bytes 1572868
  5.2 1.0 %copy-start.4 = (bf16[64,4096]{1,0:T(8,128)(2,1)S(1)}, bf16[64,4096]{1,0:T(8,128)(2,1)}, u32[]{:S(2)}) copy-start(bf16[64,4096]{1,0:T(8,128)(2,1)} %gate.1) | copy-start | bytes 1572868
  6.2 0.7 copy-start.5
  6.9 0.7 copy-start.6

commit v2 on v1

v2 whole, which is shorter than its diff:
```python
import functools

import jax
import jax.numpy as jnp
from jax import lax
from jax.experimental import pallas as pl
from jax.experimental.pallas import tpu as pltpu
from jax.sharding import PartitionSpec as P

NS_STEPS = 5
DH = 512
HEADS = 8
SCALE = DH ** (-0.5)
COEF_A, COEF_B, COEF_C = 3.4445, -4.775, 2.0315
F32, BF16 = jnp.float32, jnp.bfloat16
NT = (((1,), (1,)), ((), ()))
TN = (((0,), (0,)), ((), ()))
NN = (((1,), (0,)), ((), ()))


def mat(left, right, dims=NN):
    return lax.dot_general(left, right, dims, preferred_element_type=F32)


SCHEDULE = (
    ("grad_two", 0), ("greet", 0), ("core_send", 2), ("query_send", 0), ("grad_hidden", 0), ("x_send", 2),
    ("grad_one_three", 0), ("core_send", 0), ("grad_one_three", 1), ("core_send", 1), ("x_send", 0), ("x_send", 1),
    ("z_send", 2), ("z_send", 0), ("z_send", 1), ("readout", 0), ("y_send", 0), ("a_send", 2), ("y_send", 1),
    ("a_send", 0), ("a_send", 1), ("read_send", 0), ("f_send", 2), ("normalise", 2), ("orthogonal", 2),
    ("orthogonal", 2), ("orthogonal", 2), ("f_send", 0), ("orthogonal", 2), ("orthogonal", 2), ("orthogonal", 2),
    ("orthogonal", 2), ("orthogonal", 2), ("orthogonal", 2), ("orthogonal", 2), ("orthogonal", 2), ("orthogonal", 2),
    ("f_send", 1), ("orthogonal", 2), ("orthogonal", 2), ("orthogonal", 2), ("update", 2), ("normalise", 0),
    ("normalise", 1), ("orthogonal", 0), ("orthogonal", 1), ("orthogonal", 0), ("orthogonal", 1), ("orthogonal", 0),
    ("orthogonal", 1), ("orthogonal", 0), ("orthogonal", 1), ("orthogonal", 0), ("orthogonal", 1), ("orthogonal", 0),
    ("orthogonal", 1), ("finish_read", 0), ("orthogonal", 0), ("orthogonal", 1), ("orthogonal", 0), ("orthogonal", 1),
    ("orthogonal", 0), ("orthogonal", 1), ("orthogonal", 0), ("orthogonal", 1), ("orthogonal", 0), ("orthogonal", 1),
    ("orthogonal", 0), ("orthogonal", 1), ("orthogonal", 0), ("orthogonal", 1), ("orthogonal", 0), ("orthogonal", 1),
    ("orthogonal", 0), ("orthogonal", 1), ("update", 0), ("update", 1),
)
Z_SCATTER = (0, 1)
HALVES = (slice(0, 256), slice(256, 512))


def orthogonal_step(m, phase, x_it, gram, poly):
    low, high = HALVES
    if phase == 0:
        gram[m, :, low] = mat(x_it[m], x_it[m, low, :], NT).astype(BF16)
        gram[m, high, high] = mat(x_it[m, high], x_it[m, high, :], NT).astype(BF16)
        gram[m, low, high] = gram[m, high, low].T
    elif phase == 1:
        poly[m, :, low] = (
            COEF_B * gram[m, :, low].astype(F32) + COEF_C * mat(gram[m], gram[m, :, low])
        ).astype(BF16)
        poly[m, high, high] = (
            COEF_B * gram[m, high, high].astype(F32) + COEF_C * mat(gram[m, high], gram[m, :, high])
        ).astype(BF16)
        poly[m, low, high] = poly[m, high, low].T
    else:
        for cols in HALVES:
            x_it[m, :, cols] = (
                COEF_A * x_it[m, :, cols].astype(F32) + mat(poly[m], x_it[m, :, cols])
            ).astype(BF16)


def memory_kernel(
    schedule, z_scatter, keys, values, rates, queries, weights, gate, gain,
    layer_out, new_weights,
    k_v, v_v, w_v, rate_v, gate_v, gain_v, q_buf, r_out, r_in,
    loc, c_recv, part, x_recv, z_buf, z_part, z_recv, full, x_it, gram, poly, dg_v,
    in_sem, q_ss, q_rs, r_ss, r_rs, c_ss, c_rs, x_ss, x_rs, z_ss, z_rs, y_ss, y_rs, a_ss, a_rs, f_ss, f_rs,
):
    ctx, head = lax.axis_index("ctx"), lax.axis_index("head")
    xi, zi, core = ctx // 8, (ctx // 2) % 4, ctx % 2

    def at(x, z, c):
        return (x * 8 + z * 2 + c, head)

    def x_other(d):
        return (xi + d) % 4

    def z_other(d):
        return (zi + d) % 4

    sibling = at(xi, zi, 1 - core)
    heads_other = [(head + d) % HEADS for d in range(1, HEADS)]

    def remote(src, dst, ss, rs, target):
        return pltpu.make_async_remote_copy(
            src_ref=src, dst_ref=dst, send_sem=ss, recv_sem=rs,
            device_id=target, device_id_type=pl.DeviceIdType.MESH,
        )

    barrier = pltpu.get_barrier_semaphore()
    partners = [sibling] + [at(x_other(d), zi, core) for d in (1, 2, 3)]
    partners += [at(xi, z_other(d), core) for d in (1, 2, 3)] + [(ctx, h) for h in heads_other]
    for partner in partners:
        pl.semaphore_signal(barrier, inc=1, device_id=partner, device_id_type=pl.DeviceIdType.MESH)

    loads = [
        pltpu.make_async_copy(keys, k_v, in_sem.at[0]),
        pltpu.make_async_copy(weights.at[0, 0], w_v.at[0], in_sem.at[1]),
        pltpu.make_async_copy(weights.at[0, 1], w_v.at[1], in_sem.at[2]),
        pltpu.make_async_copy(values, v_v, in_sem.at[3]),
        pltpu.make_async_copy(weights.at[0, 2], w_v.at[2], in_sem.at[4]),
        pltpu.make_async_copy(
            queries.at[:, pl.ds(pl.multiple_of(head * DH, DH), DH)], q_buf.at[head], in_sem.at[5]
        ),
        pltpu.make_async_copy(gate, gate_v, in_sem.at[6]),
        pltpu.make_async_copy(rates, rate_v, in_sem.at[7]),
        pltpu.make_async_copy(gain, gain_v, in_sem.at[8]),
    ]
    for load in loads:
        load.start()

    live, copies = {}, {}

    def greet(_):
        pl.semaphore_wait(barrier, len(partners))

    def grad_two(_):
        loads[0].wait()
        loads[1].wait()
        g_one = mat(k_v[...], w_v[0]) * SCALE
        loads[2].wait()
        g_three = mat(k_v[...], w_v[1]) * SCALE
        sig = jax.nn.sigmoid(g_one)
        hidden = (g_one * sig * g_three).astype(BF16)
        loads[3].wait()
        loads[7].wait()
        rate_col = jnp.broadcast_to(rate_v[...], (128, DH)).T
        rate_wide = jnp.concatenate([rate_col] * 4, axis=1)
        grad_out = (-(rate_wide * v_v[...].astype(F32))).astype(BF16)
        loc[2] = (mat(hidden, grad_out, TN) * SCALE).astype(BF16)
        live.update(g_one=g_one, g_three=g_three, sig=sig, grad_out=grad_out)

    def grad_hidden(_):
        loads[4].wait()
        g_one, sig = live["g_one"], live["sig"]
        d_hidden = mat(live["grad_out"], w_v[2], NT) * SCALE
        dg_v[0] = (d_hidden * live["g_three"] * sig * (1.0 + g_one * (1.0 - sig))).astype(BF16)
        dg_v[1] = (d_hidden * (g_one * sig)).astype(BF16)

    def grad_one_three(m):
        loc[m] = (mat(k_v[...], dg_v[m], TN) * SCALE).astype(BF16)

    def start(key, copy):
        copy.start()
        copies.setdefault(key, []).append(copy)

    def arrived(key):
        for copy in copies[key]:
            copy.wait_recv()

    def core_send(m):
        start(("c", m), remote(
            loc.at[m, pl.ds(pl.multiple_of((1 - core) * 256, 256), 256)], c_recv.at[m],
            c_ss.at[m], c_rs.at[m], sibling,
        ))

    def x_send(m):
        arrived(("c", m))
        mine = loc[m, pl.ds(pl.multiple_of(core * 256, 256), 256), :].astype(F32)
        part[m] = (mine + c_recv[m].astype(F32)).astype(BF16).reshape(4, 64, DH)
        for d in (1, 3, 2):
            start(("x", m), remote(
                part.at[m, x_other(d)], x_recv.at[m, d - 1], x_ss.at[m, d - 1], x_rs.at[m, d - 1],
                at(x_other(d), zi, core),
            ))

    def z_send(m):
        arrived(("x", m))
        total = part[m, xi].astype(F32)
        for d in range(3):
            total = total + x_recv[m, d].astype(F32)
        if m in z_scatter:
            z_part[m] = total.astype(BF16).reshape(4, 16, DH)
        else:
            z_buf[m, zi] = total.astype(BF16).reshape(4, 16, DH)
        for d in (1, 3, 2):
            if m in z_scatter:
                source, target = z_part.at[m, z_other(d)], z_recv.at[m, d - 1]
            else:
                source, target = z_buf.at[m, zi], z_buf.at[m, zi]
            start(("z", m), remote(source, target, z_ss.at[m, d - 1], z_rs.at[m, d - 1], at(xi, z_other(d), core)))

    def y_send(m):
        arrived(("z", m))
        total = z_part[m, zi].astype(F32)
        for d in range(3):
            total = total + z_recv[m, d].astype(F32)
        full[m, core, xi, zi] = total.astype(BF16)
        block = full.at[m, core, xi, zi]
        for d in (1, 3, 2):
            start(("y", m), remote(block, block, y_ss.at[m, d - 1], y_rs.at[m, d - 1], at(xi, z_other(d), core)))

    def a_send(m):
        if m in z_scatter:
            arrived(("y", m))
        else:
            arrived(("z", m))
            total = z_buf[m, 0].astype(F32)
            for z in range(1, 4):
                total = total + z_buf[m, z].astype(F32)
            full[m, core, xi] = total.astype(BF16)
        block = full.at[m, core, xi]
        for d in (1, 3, 2):
            start(("a", m), remote(block, block, a_ss.at[m, d - 1], a_rs.at[m, d - 1], at(x_other(d), zi, core)))
        start(("f", m), remote(block, block, f_ss.at[m, 0], f_rs.at[m, 0], sibling))

    def f_send(m):
        for i, d in enumerate((1, 3, 2)):
            copies["a", m][i].wait_recv()
            block = full.at[m, core, (xi + 4 - d) % 4]
            start(("f", m), remote(block, block, f_ss.at[m, d], f_rs.at[m, d], sibling))

    def normalise(m):
        arrived(("f", m))
        grad = full[m].reshape(DH, DH).astype(F32)
        norm = jnp.sqrt(jnp.sum(grad * grad)) + 1e-07
        x_it[m] = (grad / norm).astype(BF16)

    def update(m):
        step_size = 0.4 * DH ** 0.5
        new_weights[0, m] = (w_v[m].astype(F32) - step_size * x_it[m].astype(F32)).astype(BF16)

    def query_send(_):
        for d, h in enumerate(heads_other):
            start("q", remote(
                queries.at[:, pl.ds(pl.multiple_of(h * DH, DH), DH)], q_buf.at[head], q_ss.at[d], q_rs.at[d], (ctx, h)
            ))

    def readout(_):
        loads[5].wait()
        arrived("q")
        q_rows = q_buf[...].reshape(HEADS * 64, DH)
        r_one = mat(q_rows, w_v[0]) * SCALE
        r_three = mat(q_rows, w_v[1]) * SCALE
        hq = (r_one * jax.nn.sigmoid(r_one) * r_three).astype(BF16)
        r_out[...] = (mat(hq, w_v[2]) * SCALE).astype(BF16).reshape(HEADS, 64, DH)

    def read_send(_):
        for d, h in enumerate(heads_other):
            start("r", remote(r_out.at[h], r_in.at[head], r_ss.at[d], r_rs.at[d], (ctx, h)))
        r_in[head] = r_out[head]

    def finish_read(_):
        loads[6].wait()
        loads[8].wait()
        arrived("r")
        for h in range(HEADS):
            cols = slice(h * DH, (h + 1) * DH)
            read = r_in[h].astype(F32)
            mean_sq = jnp.mean(read * read, axis=-1, keepdims=True)
            gated = gate_v[:, cols].astype(F32)
            layer_out[:, cols] = (
                read * lax.rsqrt(mean_sq + 1e-06) * gain_v[:, cols] * (gated * jax.nn.sigmoid(gated))
            ).astype(BF16)

    work = {
        "greet": greet, "grad_two": grad_two, "grad_hidden": grad_hidden, "grad_one_three": grad_one_three, "core_send": core_send, "x_send": x_send, "z_send": z_send,
        "y_send": y_send, "a_send": a_send, "f_send": f_send, "normalise": normalise, "update": update, "query_send": query_send, "readout": readout,
        "read_send": read_send, "finish_read": finish_read,
    }
    steps = {0: 0, 1: 0, 2: 0}
    for name, m in schedule:
        if name == "orthogonal":
            orthogonal_step(m, steps[m] % 3, x_it, gram, poly)
            steps[m] += 1
        else:
            work[name](m)

    for group in copies.values():
        for copy in group:
            copy.wait_send()


def local(keys, values, rates, queries, fast_weights, gate, gain):
    hbm = pl.BlockSpec(memory_space=pltpu.HBM)
    vmem = pl.BlockSpec(memory_space=pltpu.VMEM)
    dma = pltpu.SemaphoreType.DMA
    return pl.pallas_call(
        functools.partial(memory_kernel, SCHEDULE, Z_SCATTER),
        name="memory_layer",
        out_shape=(
            jax.ShapeDtypeStruct((64, HEADS * DH), BF16),
            jax.ShapeDtypeStruct((1, 3, DH, DH), BF16),
        ),
        in_specs=[hbm] * 7,
        out_specs=(vmem, vmem),
        scratch_shapes=[
            pltpu.VMEM((512, DH), BF16),
            pltpu.VMEM((512, DH), BF16),
            pltpu.VMEM((3, DH, DH), BF16),
            pltpu.VMEM((1, 512), F32),
            pltpu.VMEM((64, HEADS * DH), BF16),
            pltpu.VMEM((1, HEADS * DH), F32),
            pltpu.VMEM((HEADS, 64, DH), BF16),
            pltpu.VMEM((HEADS, 64, DH), BF16),
            pltpu.VMEM((HEADS, 64, DH), BF16),
            pltpu.VMEM((3, DH, DH), BF16),
            pltpu.VMEM((3, 256, DH), BF16),
            pltpu.VMEM((3, 4, 64, DH), BF16),
            pltpu.VMEM((3, 3, 64, DH), BF16),
            pltpu.VMEM((3, 4, 4, 16, DH), BF16),
            pltpu.VMEM((3, 4, 16, DH), BF16),
            pltpu.VMEM((3, 3, 16, DH), BF16),
            pltpu.VMEM((3, 2, 4, 4, 16, DH), BF16),
            pltpu.VMEM((3, DH, DH), BF16),
            pltpu.VMEM((3, DH, DH), BF16),
            pltpu.VMEM((3, DH, DH), BF16),
            pltpu.VMEM((2, DH, DH), BF16),
            dma((9,)),
            dma((7,)), dma((7,)), dma((7,)), dma((7,)),
            dma((3,)), dma((3,)),
            dma((3, 3)), dma((3, 3)), dma((3, 3)), dma((3, 3)), dma((3, 3)), dma((3, 3)), dma((3, 3)), dma((3, 3)),
            dma((3, 4)), dma((3, 4)),
        ],
        compiler_params=pltpu.CompilerParams(
            collective_id=0, has_side_effects=True, vmem_limit_bytes=48 * 2**20
        ),
    )(keys, values, rates, queries, fast_weights, gate, gain.reshape(1, HEADS * DH))


def solution(mesh):
    in_specs = (
        P("ctx", "head"),
        P("ctx", "head"),
        P("head", "ctx"),
        P(("ctx", "head"), None),
        P("head", None, None, None),
        P(("ctx", "head"), None),
        P(),
    )
    out_specs = (P(("ctx", "head"), None), P("head", None, None, None))
    return jax.shard_map(local, mesh=mesh, in_specs=in_specs, out_specs=out_specs, check_vma=False)
```

time: 75.9 us -> 61.7 us (0.81)
  Pallas kernels: 66 us -> 51.7 us
    pallas_call x1, Pallas kernels: 66 us -> 51.7 us  [local(): pl.pallas_call(functools.partial(memory_kernel, SCHEDULE, Z_SCATTER), nam...]
where the time goes in v2:
time: 61.7 us; the launch traced here: 61.3 us
  Pallas kernels  51.7 us (84%)
  local copies, waits for them, and re-layouts  8.9 us (14%)
  between operations  0.66 us (1%)
    pallas_call x1, Pallas kernels, local(): pl.pallas_call(functools.partial(memory_kernel, SCHEDULE, Z_SCATTER), nam...  51.7 us
    unnamed x16, local copies, waits for them, and re-layouts  8.9 us

profile of v2, /device:TPU:1, one launch (start us, length us, event | category | flops | bytes accessed | tf_op | source)
XLA Modules:
  0.0 61.3 jit_solution(6372927648678648919)
XLA Ops:
  0.6 0.0 copy-start
  0.6 1.4 %copy-done = bf16[1,3,512,512]{3,2,1,0:T(8,128)(2,1)S(1)} copy-done((bf16[1,3,512,512]{3,2,1,0:T(8,128)(2,1)S(1)}, bf16[1,3,512,512]{3,2,1,0:T(8,128)(2,1)}, u32[]{:S(2)}) %copy-start) | copy-done | bytes 1572888
  2.0 0.0 copy-start.1
  2.0 1.0 %copy-done.1 = bf16[512,512]{1,0:T(8,128)(2,1)S(1)} copy-done((bf16[512,512]{1,0:T(8,128)(2,1)S(1)}, bf16[512,512]{1,0:T(8,128)(2,1)}, u32[]{:S(2)}) %copy-start.1) | copy-done | bytes 524312
  3.1 0.0 copy-start.2
  3.1 1.0 %copy-done.2 = bf16[512,512]{1,0:T(8,128)(2,1)S(1)} copy-done((bf16[512,512]{1,0:T(8,128)(2,1)S(1)}, bf16[512,512]{1,0:T(8,128)(2,1)}, u32[]{:S(2)}) %copy-start.2) | copy-done | bytes 524312
  4.1 0.0 copy-start.3
  4.1 1.0 %copy-done.3 = bf16[64,4096]{1,0:T(8,128)(2,1)S(1)} copy-done((bf16[64,4096]{1,0:T(8,128)(2,1)S(1)}, bf16[64,4096]{1,0:T(8,128)(2,1)}, u32[]{:S(2)}) %copy-start.3) | copy-done | bytes 524312
  5.2 0.0 copy-start.4
  5.2 1.0 %copy-done.4 = bf16[64,4096]{1,0:T(8,128)(2,1)S(1)} copy-done((bf16[64,4096]{1,0:T(8,128)(2,1)S(1)}, bf16[64,4096]{1,0:T(8,128)(2,1)}, u32[]{:S(2)}) %copy-start.4) | copy-done | bytes 524312
  6.2 0.0 copy-start.5
  6.2 0.7 %copy-done.5 = f32[4096]{0:T(1024)S(1)} copy-done((f32[4096]{0:T(1024)S(1)}, f32[4096]{0:T(1024)}, u32[]{:S(2)}) %copy-start.5) | copy-done | bytes 16408
  6.9 0.0 copy-start.6
  6.9 0.7 %copy-done.6 = f32[1,512]{1,0:T(1,128)S(1)} copy-done((f32[1,512]{1,0:T(1,128)S(1)}, f32[1,512]{1,0:T(1,128)}, u32[]{:S(2)}) %copy-start.6) | copy-done | bytes 2072
  7.6 51.7 %memory_layer.1 = (bf16[64,4096]{1,0:T(8,128)(2,1)S(1)}, bf16[1,3,512,512]{3,2,1,0:T(8,128)(2,1)S(1)}) custom-call(bf16[512,512]{1,0:T(8,128)(2,1)S(1)} %copy-done.1, bf16[512,512]{1,0:T(8,128)(2,1)S(1)} %copy-done.2, f32[1,512]{1,0:T(1,128)S(1)} %copy-done.6, bf16[64,4096]{1,0:T(8,128)(2,1)S(1)} %copy-done.3, bf16[1,3,512,512]{3,2,1,0:T(8,128)(2,1)S(1)} %copy-done, ...), custom_call_target="tpu_custom_call" | custom-call | tf_op jit(solution)/shard_map/memory_layer/pallas_call | solution.py:281
  59.4 0.8 %copy.11 = bf16[64,4096]{1,0:T(8,128)(2,1)} copy(bf16[64,4096]{1,0:T(8,128)(2,1)S(1)} %get-tuple-element.4) | data formatting | bytes 1048576
  60.2 1.1 %copy.12 = bf16[1,3,512,512]{3,2,1,0:T(8,128)(2,1)} copy(bf16[1,3,512,512]{3,2,1,0:T(8,128)(2,1)S(1)} %get-tuple-element.5) | data formatting | bytes 3145728
Async XLA Ops:
  0.6 1.4 %copy-start = (bf16[1,3,512,512]{3,2,1,0:T(8,128)(2,1)S(1)}, bf16[1,3,512,512]{3,2,1,0:T(8,128)(2,1)}, u32[]{:S(2)}) copy-start(bf16[1,3,512,512]{3,2,1,0:T(8,128)(2,1)} %weights.1) | copy-start | bytes 4718596
  2.0 1.0 %copy-start.1 = (bf16[512,512]{1,0:T(8,128)(2,1)S(1)}, bf16[512,512]{1,0:T(8,128)(2,1)}, u32[]{:S(2)}) copy-start(bf16[512,512]{1,0:T(8,128)(2,1)} %keys.1) | copy-start | bytes 1572868
  3.1 1.0 %copy-start.2 = (bf16[512,512]{1,0:T(8,128)(2,1)S(1)}, bf16[512,512]{1,0:T(8,128)(2,1)}, u32[]{:S(2)}) copy-start(bf16[512,512]{1,0:T(8,128)(2,1)} %values.1) | copy-start | bytes 1572868
  4.1 1.0 %copy-start.3 = (bf16[64,4096]{1,0:T(8,128)(2,1)S(1)}, bf16[64,4096]{1,0:T(8,128)(2,1)}, u32[]{:S(2)}) copy-start(bf16[64,4096]{1,0:T(8,128)(2,1)} %queries.1) | copy-start | bytes 1572868
  5.2 1.0 %copy-start.4 = (bf16[64,4096]{1,0:T(8,128)(2,1)S(1)}, bf16[64,4096]{1,0:T(8,128)(2,1)}, u32[]{:S(2)}) copy-start(bf16[64,4096]{1,0:T(8,128)(2,1)} %gate.1) | copy-start | bytes 1572868
  6.2 0.7 %copy-start.5 = (f32[4096]{0:T(1024)S(1)}, f32[4096]{0:T(1024)}, u32[]{:S(2)}) copy-start(f32[4096]{0:T(1024)} %param.13) | copy-start | bytes 49156
  6.9 0.7 %copy-start.6 = (f32[1,512]{1,0:T(1,128)S(1)}, f32[1,512]{1,0:T(1,128)}, u32[]{:S(2)}) copy-start(f32[1,512]{1,0:T(1,128)} %rates.1) | copy-start | bytes 6148

commit v3 on v2

--- a/solution.py
+++ b/solution.py
@@ -12,6 +12,7 @@
 HEADS = 8
 SCALE = DH ** (-0.5)
 COEF_A, COEF_B, COEF_C = 3.4445, -4.775, 2.0315
+STEP_SIZE = 0.4 * DH ** 0.5
 F32, BF16 = jnp.float32, jnp.bfloat16
 NT = (((1,), (1,)), ((), ()))
 TN = (((0,), (0,)), ((), ()))
@@ -25,19 +26,17 @@
 SCHEDULE = (
     ("grad_two", 0), ("greet", 0), ("core_send", 2), ("query_send", 0), ("grad_hidden", 0), ("x_send", 2),
     ("grad_one_three", 0), ("core_send", 0), ("grad_one_three", 1), ("core_send", 1), ("x_send", 0), ("x_send", 1),
-    ("z_send", 2), ("z_send", 0), ("z_send", 1), ("readout", 0), ("y_send", 0), ("a_send", 2), ("y_send", 1),
-    ("a_send", 0), ("a_send", 1), ("read_send", 0), ("f_send", 2), ("normalise", 2), ("orthogonal", 2),
-    ("orthogonal", 2), ("orthogonal", 2), ("f_send", 0), ("orthogonal", 2), ("orthogonal", 2), ("orthogonal", 2),
-    ("orthogonal", 2), ("orthogonal", 2), ("orthogonal", 2), ("orthogonal", 2), ("orthogonal", 2), ("orthogonal", 2),
-    ("f_send", 1), ("orthogonal", 2), ("orthogonal", 2), ("orthogonal", 2), ("update", 2), ("normalise", 0),
-    ("normalise", 1), ("orthogonal", 0), ("orthogonal", 1), ("orthogonal", 0), ("orthogonal", 1), ("orthogonal", 0),
-    ("orthogonal", 1), ("orthogonal", 0), ("orthogonal", 1), ("orthogonal", 0), ("orthogonal", 1), ("orthogonal", 0),
-    ("orthogonal", 1), ("finish_read", 0), ("orthogonal", 0), ("orthogonal", 1), ("orthogonal", 0), ("orthogonal", 1),
-    ("orthogonal", 0), ("orthogonal", 1), ("orthogonal", 0), ("orthogonal", 1), ("orthogonal", 0), ("orthogonal", 1),
-    ("orthogonal", 0), ("orthogonal", 1), ("orthogonal", 0), ("orthogonal", 1), ("orthogonal", 0), ("orthogonal", 1),
-    ("orthogonal", 0), ("orthogonal", 1), ("update", 0), ("update", 1),
+    ("z_send", 2), ("z_send", 0), ("z_send", 1), ("readout", 0), ("y_send", 2), ("y_send", 0), ("y_send", 1),
+    ("read_send", 0), ("a_send", 2), ("a_send", 0), ("a_send", 1), ("forward_two", 2), ("normalise", 0),
+    ("orthogonal", 0), ("orthogonal", 0), ("orthogonal", 0), ("orthogonal", 0), ("orthogonal", 0), ("orthogonal", 0),
+    ("orthogonal", 0), ("orthogonal", 0), ("orthogonal", 0), ("orthogonal", 0), ("orthogonal", 0), ("orthogonal", 0),
+    ("orthogonal", 0), ("orthogonal", 0), ("orthogonal", 0), ("update", 0), ("read_wait", 0), ("finish_read", 0),
+    ("finish_read", 1), ("finish_read", 2), ("finish_read", 3), ("finish_read", 4), ("finish_read", 5),
+    ("finish_read", 6), ("finish_read", 7), ("forward_other", 0), ("normalise", 1), ("orthogonal", 1),
+    ("orthogonal", 1), ("orthogonal", 1), ("orthogonal", 1), ("orthogonal", 1), ("orthogonal", 1), ("orthogonal", 1),
+    ("orthogonal", 1), ("orthogonal", 1), ("orthogonal", 1), ("orthogonal", 1), ("orthogonal", 1), ("orthogonal", 1),
+    ("orthogonal", 1), ("update_own", 0), ("update_own", 1),
 )
-Z_SCATTER = (0, 1)
 HALVES = (slice(0, 256), slice(256, 512))
 
 
@@ -63,11 +62,11 @@
 
 
 def memory_kernel(
-    schedule, z_scatter, keys, values, rates, queries, weights, gate, gain,
+    schedule, keys, values, rates, queries, weights, gate, gain,
     layer_out, new_weights,
-    k_v, v_v, w_v, rate_v, gate_v, gain_v, q_buf, r_out, r_in,
-    loc, c_recv, part, x_recv, z_buf, z_part, z_recv, full, x_it, gram, poly, dg_v,
-    in_sem, q_ss, q_rs, r_ss, r_rs, c_ss, c_rs, x_ss, x_rs, z_ss, z_rs, y_ss, y_rs, a_ss, a_rs, f_ss, f_rs,
+    k_v, v_v, w_v, rate_v, gate_v, gain_v, q_buf, r_out, r_in, layer_v, new_v,
+    loc, c_recv, part, x_recv, z_part, z_recv, full, x_it, gram, poly, dg_v,
+    in_sem, q_ss, q_rs, r_ss, r_rs, c_ss, c_rs, x_ss, x_rs, z_ss, z_rs, y_ss, y_rs, a_ss, a_rs, f_ss, f_rs, e_ss, e_rs, out_sem,
 ):
     ctx, head = lax.axis_index("ctx"), lax.axis_index("head")
     xi, zi, core = ctx // 8, (ctx // 2) % 4, ctx % 2
@@ -112,7 +111,7 @@
     for load in loads:
         load.start()
 
-    live, copies = {}, {}
+    live, copies, stores = {}, {}, []
 
     def greet(_):
         pl.semaphore_wait(barrier, len(partners))
@@ -147,6 +146,11 @@
         copy.start()
         copies.setdefault(key, []).append(copy)
 
+    def store(source, target, i):
+        copy = pltpu.make_async_copy(source, target, out_sem.at[i])
+        copy.start()
+        stores.append(copy)
+
     def arrived(key):
         for copy in copies[key]:
             copy.wait_recv()
@@ -172,16 +176,12 @@
         total = part[m, xi].astype(F32)
         for d in range(3):
             total = total + x_recv[m, d].astype(F32)
-        if m in z_scatter:
-            z_part[m] = total.astype(BF16).reshape(4, 16, DH)
-        else:
-            z_buf[m, zi] = total.astype(BF16).reshape(4, 16, DH)
+        z_part[m] = total.astype(BF16).reshape(4, 16, DH)
         for d in (1, 3, 2):
-            if m in z_scatter:
-                source, target = z_part.at[m, z_other(d)], z_recv.at[m, d - 1]
-            else:
-                source, target = z_buf.at[m, zi], z_buf.at[m, zi]
-            start(("z", m), remote(source, target, z_ss.at[m, d - 1], z_rs.at[m, d - 1], at(xi, z_other(d), core)))
+            start(("z", m), remote(
+                z_part.at[m, z_other(d)], z_recv.at[m, d - 1], z_ss.at[m, d - 1], z_rs.at[m, d - 1],
+                at(xi, z_other(d), core),
+            ))
 
     def y_send(m):
         arrived(("z", m))
@@ -194,34 +194,43 @@
             start(("y", m), remote(block, block, y_ss.at[m, d - 1], y_rs.at[m, d - 1], at(xi, z_other(d), core)))
 
     def a_send(m):
-        if m in z_scatter:
-            arrived(("y", m))
-        else:
-            arrived(("z", m))
-            total = z_buf[m, 0].astype(F32)
-            for z in range(1, 4):
-                total = total + z_buf[m, z].astype(F32)
-            full[m, core, xi] = total.astype(BF16)
+        arrived(("y", m))
         block = full.at[m, core, xi]
         for d in (1, 3, 2):
             start(("a", m), remote(block, block, a_ss.at[m, d - 1], a_rs.at[m, d - 1], at(x_other(d), zi, core)))
-        start(("f", m), remote(block, block, f_ss.at[m, 0], f_rs.at[m, 0], sibling))
-
-    def f_send(m):
+        if m == 2:
+            start(("f", m), remote(block, block, f_ss.at[0], f_rs.at[0], sibling))
+
+    def forward_two(_):
         for i, d in enumerate((1, 3, 2)):
-            copies["a", m][i].wait_recv()
-            block = full.at[m, core, (xi + 4 - d) % 4]
-            start(("f", m), remote(block, block, f_ss.at[m, d], f_rs.at[m, d], sibling))
-
-    def normalise(m):
-        arrived(("f", m))
-        grad = full[m].reshape(DH, DH).astype(F32)
+            copies["a", 2][i].wait_recv()
+            block = full.at[2, core, (xi + 4 - d) % 4]
+            start(("f", 2), remote(block, block, f_ss.at[d], f_rs.at[d], sibling))
+
+    def forward_other(_):
+        arrived(("a", 0))
+        arrived(("a", 1))
+        block = full.at[1 - core, core]
+        start("e", remote(block, block, e_ss.at[0], e_rs.at[0], sibling))
+
+    def normalise(slot):
+        arrived(("f", 2) if slot == 0 else "e")
+        grad = full[2 if slot == 0 else core].reshape(DH, DH).astype(F32)
         norm = jnp.sqrt(jnp.sum(grad * grad)) + 1e-07
-        x_it[m] = (grad / norm).astype(BF16)
-
-    def update(m):
-        step_size = 0.4 * DH ** 0.5
-        new_weights[0, m] = (w_v[m].astype(F32) - step_size * x_it[m].astype(F32)).astype(BF16)
+        x_it[slot] = (grad / norm).astype(BF16)
+
+    def update(_):
+        new_v[2] = (w_v[2].astype(F32) - STEP_SIZE * x_it[0].astype(F32)).astype(BF16)
+        store(new_v.at[2], new_weights.at[0, 2], 0)
+
+    def update_own(half):
+        cols = HALVES[half]
+        last = (COEF_A * x_it[1, :, cols].astype(F32) + mat(poly[1], x_it[1, :, cols])).astype(BF16)
+        new_v[core, :, cols] = (w_v[core, :, cols].astype(F32) - STEP_SIZE * last.astype(F32)).astype(BF16)
+        block = new_v.at[core, :, cols]
+        target = new_weights.at[0, core, :, cols]
+        start("e", remote(block, target, e_ss.at[1 + half], e_rs.at[1 + half], sibling))
+        store(block, target, 1 + half)
 
     def query_send(_):
         for d, h in enumerate(heads_other):
@@ -243,25 +252,28 @@
             start("r", remote(r_out.at[h], r_in.at[head], r_ss.at[d], r_rs.at[d], (ctx, h)))
         r_in[head] = r_out[head]
 
-    def finish_read(_):
+    def read_wait(_):
         loads[6].wait()
         loads[8].wait()
         arrived("r")
-        for h in range(HEADS):
-            cols = slice(h * DH, (h + 1) * DH)
-            read = r_in[h].astype(F32)
-            mean_sq = jnp.mean(read * read, axis=-1, keepdims=True)
-            gated = gate_v[:, cols].astype(F32)
-            layer_out[:, cols] = (
-                read * lax.rsqrt(mean_sq + 1e-06) * gain_v[:, cols] * (gated * jax.nn.sigmoid(gated))
-            ).astype(BF16)
+
+    def finish_read(h):
+        cols = slice(h * DH, (h + 1) * DH)
+        read = r_in[h].astype(F32)
+        mean_sq = jnp.mean(read * read, axis=-1, keepdims=True)
+        gated = gate_v[:, cols].astype(F32)
+        layer_v[:, cols] = (
+            read * lax.rsqrt(mean_sq + 1e-06) * gain_v[:, cols] * (gated * jax.nn.sigmoid(gated))
+        ).astype(BF16)
+        if h == HEADS - 1:
+            store(layer_v, layer_out, 3)
 
     work = {
         "greet": greet, "grad_two": grad_two, "grad_hidden": grad_hidden, "grad_one_three": grad_one_three, "core_send": core_send, "x_send": x_send, "z_send": z_send,
-        "y_send": y_send, "a_send": a_send, "f_send": f_send, "normalise": normalise, "update": update, "query_send": query_send, "readout": readout,
+        "y_send": y_send, "a_send": a_send, "forward_two": forward_two, "forward_other": forward_other, "normalise": normalise, "update": update, "update_own": update_own, "read_wait": read_wait, "query_send": query_send, "readout": readout,
         "read_send": read_send, "finish_read": finish_read,
     }
-    steps = {0: 0, 1: 0, 2: 0}
+    steps = [0, 0]
     for name, m in schedule:
         if name == "orthogonal":
             orthogonal_step(m, steps[m] % 3, x_it, gram, poly)
@@ -269,24 +281,27 @@
         else:
             work[name](m)
 
+    for copy in copies["e"][1:]:
+        copy.wait_recv()
     for group in copies.values():
         for copy in group:
             copy.wait_send()
+    for copy in stores:
+        copy.wait()
 
 
 def local(keys, values, rates, queries, fast_weights, gate, gain):
     hbm = pl.BlockSpec(memory_space=pltpu.HBM)
-    vmem = pl.BlockSpec(memory_space=pltpu.VMEM)
     dma = pltpu.SemaphoreType.DMA
     return pl.pallas_call(
-        functools.partial(memory_kernel, SCHEDULE, Z_SCATTER),
+        functools.partial(memory_kernel, SCHEDULE),
         name="memory_layer",
         out_shape=(
             jax.ShapeDtypeStruct((64, HEADS * DH), BF16),
             jax.ShapeDtypeStruct((1, 3, DH, DH), BF16),
         ),
         in_specs=[hbm] * 7,
-        out_specs=(vmem, vmem),
+        out_specs=(hbm, hbm),
         scratch_shapes=[
             pltpu.VMEM((512, DH), BF16),
             pltpu.VMEM((512, DH), BF16),
@@ -297,26 +312,27 @@
             pltpu.VMEM((HEADS, 64, DH), BF16),
             pltpu.VMEM((HEADS, 64, DH), BF16),
             pltpu.VMEM((HEADS, 64, DH), BF16),
+            pltpu.VMEM((64, HEADS * DH), BF16),
+            pltpu.VMEM((3, DH, DH), BF16),
             pltpu.VMEM((3, DH, DH), BF16),
             pltpu.VMEM((3, 256, DH), BF16),
             pltpu.VMEM((3, 4, 64, DH), BF16),
             pltpu.VMEM((3, 3, 64, DH), BF16),
-            pltpu.VMEM((3, 4, 4, 16, DH), BF16),
             pltpu.VMEM((3, 4, 16, DH), BF16),
             pltpu.VMEM((3, 3, 16, DH), BF16),
             pltpu.VMEM((3, 2, 4, 4, 16, DH), BF16),
-            pltpu.VMEM((3, DH, DH), BF16),
-            pltpu.VMEM((3, DH, DH), BF16),
-            pltpu.VMEM((3, DH, DH), BF16),
+            pltpu.VMEM((2, DH, DH), BF16),
+            pltpu.VMEM((2, DH, DH), BF16),
+            pltpu.VMEM((2, DH, DH), BF16),
             pltpu.VMEM((2, DH, DH), BF16),
             dma((9,)),
             dma((7,)), dma((7,)), dma((7,)), dma((7,)),
             dma((3,)), dma((3,)),
             dma((3, 3)), dma((3, 3)), dma((3, 3)), dma((3, 3)), dma((3, 3)), dma((3, 3)), dma((3, 3)), dma((3, 3)),
-            dma((3, 4)), dma((3, 4)),
+            dma((4,)), dma((4,)), dma((3,)), dma((3,)), dma((4,)),
         ],
         compiler_params=pltpu.CompilerParams(
-            collective_id=0, has_side_effects=True, vmem_limit_bytes=48 * 2**20
+            collective_id=0, has_side_effects=True, vmem_limit_bytes=60 * 2**20
         ),
     )(keys, values, rates, queries, fast_weights, gate, gain.reshape(1, HEADS * DH))
 

time: 61.7 us -> 57.8 us (0.937)
  local copies, waits for them, and re-layouts: 8.9 us -> 4.52 us
  Pallas kernels: 51.7 us -> 52.5 us
    unnamed x16 -> x2, local copies, waits for them, and re-layouts: 8.9 us -> 4.52 us
    pallas_call x1, Pallas kernels: 51.7 us -> 52.5 us  [local(): pl.pallas_call(functools.partial(memory_kernel, SCHEDULE), name='memory_l...]
where the time goes in v3:
time: 57.8 us; the launch traced here: 57.7 us
  Pallas kernels  52.5 us (91%)
  local copies, waits for them, and re-layouts  4.52 us (8%)
  between operations  0.64 us (1%)
    pallas_call x1, Pallas kernels, local(): pl.pallas_call(functools.partial(memory_kernel, SCHEDULE), name='memory_l...  52.5 us
    unnamed x2, local copies, waits for them, and re-layouts  4.52 us

profile of v3, /device:TPU:1, one launch (start us, length us, event | category | flops | bytes accessed | tf_op | source)
XLA Modules:
  0.0 57.7 jit_solution(14079274925597721566)
XLA Ops:
  0.6 52.5 %memory_layer.1 = (bf16[64,4096]{1,0:T(8,128)(2,1)}, bf16[1,3,512,512]{3,2,1,0:T(8,128)(2,1)}) custom-call(bf16[512,512]{1,0:T(8,128)(2,1)} %keys.1, bf16[512,512]{1,0:T(8,128)(2,1)} %values.1, f32[1,512]{1,0:T(1,128)} %rates.1, bf16[64,4096]{1,0:T(8,128)(2,1)} %queries.1, bf16[1,3,512,512]{3,2,1,0:T(8,128)(2,1)} %weights.1, bf16[64,4096]{1,0:T(8,128)(2,1)} %gate.1, ...), custom_call_target="tpu_custom_call" | custom-call | tf_op jit(solution)/shard_map/memory_layer/pallas_call | solution.py:296
  53.1 1.9 %copy.11 = bf16[64,4096]{1,0:T(8,128)(2,1)} copy(bf16[64,4096]{1,0:T(8,128)(2,1)} %get-tuple-element.4) | data formatting | bytes 1048576
  55.0 2.7 %copy.12 = bf16[1,3,512,512]{3,2,1,0:T(8,128)(2,1)} copy(bf16[1,3,512,512]{3,2,1,0:T(8,128)(2,1)} %get-tuple-element.5) | data formatting | bytes 3145728

commit v4 on v3

--- a/solution.py
+++ b/solution.py
@@ -25,17 +25,17 @@
 
 SCHEDULE = (
     ("grad_two", 0), ("greet", 0), ("core_send", 2), ("query_send", 0), ("grad_hidden", 0), ("x_send", 2),
-    ("grad_one_three", 0), ("core_send", 0), ("grad_one_three", 1), ("core_send", 1), ("x_send", 0), ("x_send", 1),
+    ("grad_one_three", 0), ("core_send", 0), ("core_send", 1), ("grad_one_three", 1), ("x_send", 0), ("x_send", 1),
     ("z_send", 2), ("z_send", 0), ("z_send", 1), ("readout", 0), ("y_send", 2), ("y_send", 0), ("y_send", 1),
     ("read_send", 0), ("a_send", 2), ("a_send", 0), ("a_send", 1), ("forward_two", 2), ("normalise", 0),
     ("orthogonal", 0), ("orthogonal", 0), ("orthogonal", 0), ("orthogonal", 0), ("orthogonal", 0), ("orthogonal", 0),
     ("orthogonal", 0), ("orthogonal", 0), ("orthogonal", 0), ("orthogonal", 0), ("orthogonal", 0), ("orthogonal", 0),
     ("orthogonal", 0), ("orthogonal", 0), ("orthogonal", 0), ("update", 0), ("read_wait", 0), ("finish_read", 0),
     ("finish_read", 1), ("finish_read", 2), ("finish_read", 3), ("finish_read", 4), ("finish_read", 5),
-    ("finish_read", 6), ("finish_read", 7), ("forward_other", 0), ("normalise", 1), ("orthogonal", 1),
+    ("finish_read", 6), ("finish_read", 7), ("normalise", 1), ("orthogonal", 1), ("orthogonal", 1), ("orthogonal", 1),
     ("orthogonal", 1), ("orthogonal", 1), ("orthogonal", 1), ("orthogonal", 1), ("orthogonal", 1), ("orthogonal", 1),
-    ("orthogonal", 1), ("orthogonal", 1), ("orthogonal", 1), ("orthogonal", 1), ("orthogonal", 1), ("orthogonal", 1),
-    ("orthogonal", 1), ("update_own", 0), ("update_own", 1),
+    ("orthogonal", 1), ("orthogonal", 1), ("orthogonal", 1), ("orthogonal", 1), ("orthogonal", 1), ("update_own", 0),
+    ("update_own", 1),
 )
 HALVES = (slice(0, 256), slice(256, 512))
 
@@ -64,9 +64,9 @@
 def memory_kernel(
     schedule, keys, values, rates, queries, weights, gate, gain,
     layer_out, new_weights,
-    k_v, v_v, w_v, rate_v, gate_v, gain_v, q_buf, r_out, r_in, layer_v, new_v,
+    k_v, v_v, w_v, rate_v, gate_v, gain_v, q_buf, r_out, r_in,
     loc, c_recv, part, x_recv, z_part, z_recv, full, x_it, gram, poly, dg_v,
-    in_sem, q_ss, q_rs, r_ss, r_rs, c_ss, c_rs, x_ss, x_rs, z_ss, z_rs, y_ss, y_rs, a_ss, a_rs, f_ss, f_rs, e_ss, e_rs, out_sem,
+    in_sem, q_ss, q_rs, r_ss, r_rs, c_ss, c_rs, x_ss, x_rs, z_ss, z_rs, y_ss, y_rs, a_ss, a_rs, f_ss, f_rs, e_ss, e_rs,
 ):
     ctx, head = lax.axis_index("ctx"), lax.axis_index("head")
     xi, zi, core = ctx // 8, (ctx // 2) % 4, ctx % 2
@@ -111,7 +111,7 @@
     for load in loads:
         load.start()
 
-    live, copies, stores = {}, {}, []
+    live, copies = {}, {}
 
     def greet(_):
         pl.semaphore_wait(barrier, len(partners))
@@ -139,31 +139,32 @@
         dg_v[0] = (d_hidden * live["g_three"] * sig * (1.0 + g_one * (1.0 - sig))).astype(BF16)
         dg_v[1] = (d_hidden * (g_one * sig)).astype(BF16)
 
-    def grad_one_three(m):
+    def grad_one_three(mine):
+        m = core if mine else 1 - core
         loc[m] = (mat(k_v[...], dg_v[m], TN) * SCALE).astype(BF16)
 
     def start(key, copy):
         copy.start()
         copies.setdefault(key, []).append(copy)
 
-    def store(source, target, i):
-        copy = pltpu.make_async_copy(source, target, out_sem.at[i])
-        copy.start()
-        stores.append(copy)
-
     def arrived(key):
         for copy in copies[key]:
             copy.wait_recv()
 
+    def rows_of(piece, c):
+        if piece == 2:
+            return loc.at[2, pl.ds(pl.multiple_of(c * 256, 256), 256)]
+        return loc.at[c, pl.ds(piece * 256, 256)]
+
     def core_send(m):
-        start(("c", m), remote(
-            loc.at[m, pl.ds(pl.multiple_of((1 - core) * 256, 256), 256)], c_recv.at[m],
-            c_ss.at[m], c_rs.at[m], sibling,
-        ))
+        start(("c", m), remote(rows_of(m, 1 - core), c_recv.at[m], c_ss.at[m], c_rs.at[m], sibling))
+
+    def block_of(piece, *at_block):
+        return full.at[(0, core, *at_block) if piece == 2 else (1, piece, *at_block)]
 
     def x_send(m):
         arrived(("c", m))
-        mine = loc[m, pl.ds(pl.multiple_of(core * 256, 256), 256), :].astype(F32)
+        mine = rows_of(m, core)[...].astype(F32)
         part[m] = (mine + c_recv[m].astype(F32)).astype(BF16).reshape(4, 64, DH)
         for d in (1, 3, 2):
             start(("x", m), remote(
@@ -188,14 +189,14 @@
         total = z_part[m, zi].astype(F32)
         for d in range(3):
             total = total + z_recv[m, d].astype(F32)
-        full[m, core, xi, zi] = total.astype(BF16)
-        block = full.at[m, core, xi, zi]
+        block = block_of(m, xi, zi)
+        block[...] = total.astype(BF16)
         for d in (1, 3, 2):
             start(("y", m), remote(block, block, y_ss.at[m, d - 1], y_rs.at[m, d - 1], at(xi, z_other(d), core)))
 
     def a_send(m):
         arrived(("y", m))
-        block = full.at[m, core, xi]
+        block = block_of(m, xi)
         for d in (1, 3, 2):
             start(("a", m), remote(block, block, a_ss.at[m, d - 1], a_rs.at[m, d - 1], at(x_other(d), zi, core)))
         if m == 2:
@@ -204,33 +205,25 @@
     def forward_two(_):
         for i, d in enumerate((1, 3, 2)):
             copies["a", 2][i].wait_recv()
-            block = full.at[2, core, (xi + 4 - d) % 4]
+            block = block_of(2, (xi + 4 - d) % 4)
             start(("f", 2), remote(block, block, f_ss.at[d], f_rs.at[d], sibling))
 
-    def forward_other(_):
-        arrived(("a", 0))
-        arrived(("a", 1))
-        block = full.at[1 - core, core]
-        start("e", remote(block, block, e_ss.at[0], e_rs.at[0], sibling))
-
     def normalise(slot):
-        arrived(("f", 2) if slot == 0 else "e")
-        grad = full[2 if slot == 0 else core].reshape(DH, DH).astype(F32)
+        for key in (("f", 2),) if slot == 0 else (("a", 0), ("a", 1)):
+            arrived(key)
+        grad = full[slot].reshape(DH, DH).astype(F32)
         norm = jnp.sqrt(jnp.sum(grad * grad)) + 1e-07
         x_it[slot] = (grad / norm).astype(BF16)
 
     def update(_):
-        new_v[2] = (w_v[2].astype(F32) - STEP_SIZE * x_it[0].astype(F32)).astype(BF16)
-        store(new_v.at[2], new_weights.at[0, 2], 0)
+        new_weights[0, 2] = (w_v[2].astype(F32) - STEP_SIZE * x_it[0].astype(F32)).astype(BF16)
 
     def update_own(half):
         cols = HALVES[half]
         last = (COEF_A * x_it[1, :, cols].astype(F32) + mat(poly[1], x_it[1, :, cols])).astype(BF16)
-        new_v[core, :, cols] = (w_v[core, :, cols].astype(F32) - STEP_SIZE * last.astype(F32)).astype(BF16)
-        block = new_v.at[core, :, cols]
-        target = new_weights.at[0, core, :, cols]
-        start("e", remote(block, target, e_ss.at[1 + half], e_rs.at[1 + half], sibling))
-        store(block, target, 1 + half)
+        new_weights[0, core, :, cols] = (w_v[core, :, cols].astype(F32) - STEP_SIZE * last.astype(F32)).astype(BF16)
+        block = new_weights.at[0, core, :, cols]
+        start("e", remote(block, block, e_ss.at[half], e_rs.at[half], sibling))
 
     def query_send(_):
         for d, h in enumerate(heads_other):
@@ -262,15 +255,13 @@
         read = r_in[h].astype(F32)
         mean_sq = jnp.mean(read * read, axis=-1, keepdims=True)
         gated = gate_v[:, cols].astype(F32)
-        layer_v[:, cols] = (
+        layer_out[:, cols] = (
             read * lax.rsqrt(mean_sq + 1e-06) * gain_v[:, cols] * (gated * jax.nn.sigmoid(gated))
         ).astype(BF16)
-        if h == HEADS - 1:
-            store(layer_v, layer_out, 3)
 
     work = {
         "greet": greet, "grad_two": grad_two, "grad_hidden": grad_hidden, "grad_one_three": grad_one_three, "core_send": core_send, "x_send": x_send, "z_send": z_send,
-        "y_send": y_send, "a_send": a_send, "forward_two": forward_two, "forward_other": forward_other, "normalise": normalise, "update": update, "update_own": update_own, "read_wait": read_wait, "query_send": query_send, "readout": readout,
+        "y_send": y_send, "a_send": a_send, "forward_two": forward_two, "normalise": normalise, "update": update, "update_own": update_own, "read_wait": read_wait, "query_send": query_send, "readout": readout,
         "read_send": read_send, "finish_read": finish_read,
     }
     steps = [0, 0]
@@ -281,27 +272,26 @@
         else:
             work[name](m)
 
-    for copy in copies["e"][1:]:
-        copy.wait_recv()
+    arrived("e")
     for group in copies.values():
         for copy in group:
             copy.wait_send()
-    for copy in stores:
-        copy.wait()
 
 
 def local(keys, values, rates, queries, fast_weights, gate, gain):
+    operands = (keys, values, rates, queries, fast_weights, gate, gain.reshape(1, HEADS * DH))
+    vmem = pl.BlockSpec(memory_space=pltpu.VMEM)
     hbm = pl.BlockSpec(memory_space=pltpu.HBM)
     dma = pltpu.SemaphoreType.DMA
     return pl.pallas_call(
         functools.partial(memory_kernel, SCHEDULE),
         name="memory_layer",
         out_shape=(
-            jax.ShapeDtypeStruct((64, HEADS * DH), BF16),
-            jax.ShapeDtypeStruct((1, 3, DH, DH), BF16),
+            pltpu.VMEM((64, HEADS * DH), BF16),
+            pltpu.VMEM((1, 3, DH, DH), BF16),
         ),
         in_specs=[hbm] * 7,
-        out_specs=(hbm, hbm),
+        out_specs=(vmem, vmem),
         scratch_shapes=[
             pltpu.VMEM((512, DH), BF16),
             pltpu.VMEM((512, DH), BF16),
@@ -312,15 +302,13 @@
             pltpu.VMEM((HEADS, 64, DH), BF16),
             pltpu.VMEM((HEADS, 64, DH), BF16),
             pltpu.VMEM((HEADS, 64, DH), BF16),
-            pltpu.VMEM((64, HEADS * DH), BF16),
-            pltpu.VMEM((3, DH, DH), BF16),
             pltpu.VMEM((3, DH, DH), BF16),
             pltpu.VMEM((3, 256, DH), BF16),
             pltpu.VMEM((3, 4, 64, DH), BF16),
             pltpu.VMEM((3, 3, 64, DH), BF16),
             pltpu.VMEM((3, 4, 16, DH), BF16),
             pltpu.VMEM((3, 3, 16, DH), BF16),
-            pltpu.VMEM((3, 2, 4, 4, 16, DH), BF16),
+            pltpu.VMEM((2, 2, 4, 4, 16, DH), BF16),
             pltpu.VMEM((2, DH, DH), BF16),
             pltpu.VMEM((2, DH, DH), BF16),
             pltpu.VMEM((2, DH, DH), BF16),
@@ -329,12 +317,12 @@
             dma((7,)), dma((7,)), dma((7,)), dma((7,)),
             dma((3,)), dma((3,)),
             dma((3, 3)), dma((3, 3)), dma((3, 3)), dma((3, 3)), dma((3, 3)), dma((3, 3)), dma((3, 3)), dma((3, 3)),
-            dma((4,)), dma((4,)), dma((3,)), dma((3,)), dma((4,)),
+            dma((4,)), dma((4,)), dma((2,)), dma((2,)),
         ],
         compiler_params=pltpu.CompilerParams(
-            collective_id=0, has_side_effects=True, vmem_limit_bytes=60 * 2**20
+            collective_id=0, has_side_effects=True, vmem_limit_bytes=44 * 2**20
         ),
-    )(keys, values, rates, queries, fast_weights, gate, gain.reshape(1, HEADS * DH))
+    )(*(pltpu.with_memory_space_constraint(operand, pltpu.HBM) for operand in operands))
 
 
 def solution(mesh):

time: 57.8 us -> 53.5 us (0.926)
  local copies, waits for them, and re-layouts: 4.52 us -> 1.94 us
  Pallas kernels: 52.5 us -> 50.9 us
    unnamed x2, local copies, waits for them, and re-layouts: 4.52 us -> 1.94 us
    pallas_call x1, Pallas kernels: 52.5 us -> 50.9 us  [local(): pl.pallas_call(functools.partial(memory_kernel, SCHEDULE), name='memory_l...]
where the time goes in v4:
time: 53.5 us
  Pallas kernels  50.9 us (95%)
  local copies, waits for them, and re-layouts  1.94 us (4%)
  between operations  0.64 us (1%)
    pallas_call x1, Pallas kernels, local(): pl.pallas_call(functools.partial(memory_kernel, SCHEDULE), name='memory_l...  50.9 us
    unnamed x2, local copies, waits for them, and re-layouts  1.94 us

profile of v4, /device:TPU:1, one launch (start us, length us, event | category | flops | bytes accessed | tf_op | source)
XLA Modules:
  0.0 53.5 jit_solution(17446726646513013616)
XLA Ops:
  0.6 50.9 %memory_layer.1 = (bf16[64,4096]{1,0:T(8,128)(2,1)S(1)}, bf16[1,3,512,512]{3,2,1,0:T(8,128)(2,1)S(1)}) custom-call(bf16[512,512]{1,0:T(8,128)(2,1)} %keys.1, bf16[512,512]{1,0:T(8,128)(2,1)} %values.1, f32[1,512]{1,0:T(1,128)} %rates.1, bf16[64,4096]{1,0:T(8,128)(2,1)} %queries.1, bf16[1,3,512,512]{3,2,1,0:T(8,128)(2,1)} %weights.1, bf16[64,4096]{1,0:T(8,128)(2,1)} %gate.1, ...), custom_call_target="tpu_custom_call" | custom-call | tf_op jit(solution)/shard_map/memory_layer/pallas_call | solution.py:286
  51.5 0.8 %copy.11 = bf16[64,4096]{1,0:T(8,128)(2,1)} copy(bf16[64,4096]{1,0:T(8,128)(2,1)S(1)} %get-tuple-element.2) | data formatting | bytes 1048576
  52.3 1.1 %copy.12 = bf16[1,3,512,512]{3,2,1,0:T(8,128)(2,1)} copy(bf16[1,3,512,512]{3,2,1,0:T(8,128)(2,1)S(1)} %get-tuple-element.3) | data formatting | bytes 3145728

commit v5 on v4

--- a/solution.py
+++ b/solution.py
@@ -24,18 +24,18 @@
 
 
 SCHEDULE = (
-    ("grad_two", 0), ("greet", 0), ("core_send", 2), ("query_send", 0), ("grad_hidden", 0), ("x_send", 2),
-    ("grad_one_three", 0), ("core_send", 0), ("core_send", 1), ("grad_one_three", 1), ("x_send", 0), ("x_send", 1),
-    ("z_send", 2), ("z_send", 0), ("z_send", 1), ("readout", 0), ("y_send", 2), ("y_send", 0), ("y_send", 1),
-    ("read_send", 0), ("a_send", 2), ("a_send", 0), ("a_send", 1), ("forward_two", 2), ("normalise", 0),
+    ("grad_two", 0), ("greet", 0), ("core_send", 2), ("query_send", 0), ("grad_two", 1), ("x_send", 2),
+    ("grad_hidden", 0), ("grad_hidden", 1), ("grad_one_three", 0), ("core_send", 0), ("core_send", 1),
+    ("grad_one_three", 1), ("x_send", 0), ("x_send", 1), ("z_send", 2), ("z_send", 0), ("z_send", 1), ("readout", 0),
+    ("y_send", 2), ("y_send", 0), ("y_send", 1), ("read_send", 0), ("a_send", 2), ("a_send", 0), ("a_send", 1),
+    ("forward_two", 2), ("normalise", 0), ("orthogonal", 0), ("orthogonal", 0), ("orthogonal", 0), ("orthogonal", 0),
     ("orthogonal", 0), ("orthogonal", 0), ("orthogonal", 0), ("orthogonal", 0), ("orthogonal", 0), ("orthogonal", 0),
-    ("orthogonal", 0), ("orthogonal", 0), ("orthogonal", 0), ("orthogonal", 0), ("orthogonal", 0), ("orthogonal", 0),
-    ("orthogonal", 0), ("orthogonal", 0), ("orthogonal", 0), ("update", 0), ("read_wait", 0), ("finish_read", 0),
-    ("finish_read", 1), ("finish_read", 2), ("finish_read", 3), ("finish_read", 4), ("finish_read", 5),
-    ("finish_read", 6), ("finish_read", 7), ("normalise", 1), ("orthogonal", 1), ("orthogonal", 1), ("orthogonal", 1),
+    ("orthogonal", 0), ("orthogonal", 0), ("orthogonal", 0), ("orthogonal", 0), ("orthogonal", 0), ("update", 0),
+    ("read_wait", 0), ("finish_read", 0), ("finish_read", 1), ("finish_read", 2), ("finish_read", 3),
+    ("finish_read", 4), ("finish_read", 5), ("finish_read", 6), ("finish_read", 7), ("normalise", 1),
     ("orthogonal", 1), ("orthogonal", 1), ("orthogonal", 1), ("orthogonal", 1), ("orthogonal", 1), ("orthogonal", 1),
-    ("orthogonal", 1), ("orthogonal", 1), ("orthogonal", 1), ("orthogonal", 1), ("orthogonal", 1), ("update_own", 0),
-    ("update_own", 1),
+    ("orthogonal", 1), ("orthogonal", 1), ("orthogonal", 1), ("orthogonal", 1), ("orthogonal", 1), ("orthogonal", 1),
+    ("orthogonal", 1), ("orthogonal", 1), ("update_own", 0), ("update_own", 1),
 )
 HALVES = (slice(0, 256), slice(256, 512))
 
@@ -89,12 +89,6 @@
             device_id=target, device_id_type=pl.DeviceIdType.MESH,
         )
 
-    barrier = pltpu.get_barrier_semaphore()
-    partners = [sibling] + [at(x_other(d), zi, core) for d in (1, 2, 3)]
-    partners += [at(xi, z_other(d), core) for d in (1, 2, 3)] + [(ctx, h) for h in heads_other]
-    for partner in partners:
-        pl.semaphore_signal(barrier, inc=1, device_id=partner, device_id_type=pl.DeviceIdType.MESH)
-
     loads = [
         pltpu.make_async_copy(keys, k_v, in_sem.at[0]),
         pltpu.make_async_copy(weights.at[0, 0], w_v.at[0], in_sem.at[1]),
@@ -108,36 +102,54 @@
         pltpu.make_async_copy(rates, rate_v, in_sem.at[7]),
         pltpu.make_async_copy(gain, gain_v, in_sem.at[8]),
     ]
-    for load in loads:
-        load.start()
+    for i in (0, 1, 2, 7, 3):
+        loads[i].start()
+
+    barrier = pltpu.get_barrier_semaphore()
+    partners = [sibling] + [at(x_other(d), zi, core) for d in (1, 2, 3)]
+    partners += [at(xi, z_other(d), core) for d in (1, 2, 3)] + [(ctx, h) for h in heads_other]
+    for partner in partners:
+        pl.semaphore_signal(barrier, inc=1, device_id=partner, device_id_type=pl.DeviceIdType.MESH)
+    for i in (4, 5, 6, 8):
+        loads[i].start()
 
     live, copies = {}, {}
 
     def greet(_):
         pl.semaphore_wait(barrier, len(partners))
 
-    def grad_two(_):
-        loads[0].wait()
-        loads[1].wait()
-        g_one = mat(k_v[...], w_v[0]) * SCALE
-        loads[2].wait()
-        g_three = mat(k_v[...], w_v[1]) * SCALE
+    def columns(own):
+        half = core if own else 1 - core
+        return pl.ds(pl.multiple_of(half * 256, 256), 256)
+
+    def grad_two(own):
+        cols = columns(own)
+        if not own:
+            loads[0].wait()
+            loads[1].wait()
+        g_one = mat(k_v[...], w_v[0, :, cols]) * SCALE
+        if not own:
+            loads[2].wait()
+        g_three = mat(k_v[...], w_v[1, :, cols]) * SCALE
         sig = jax.nn.sigmoid(g_one)
         hidden = (g_one * sig * g_three).astype(BF16)
-        loads[3].wait()
-        loads[7].wait()
-        rate_col = jnp.broadcast_to(rate_v[...], (128, DH)).T
-        rate_wide = jnp.concatenate([rate_col] * 4, axis=1)
-        grad_out = (-(rate_wide * v_v[...].astype(F32))).astype(BF16)
-        loc[2] = (mat(hidden, grad_out, TN) * SCALE).astype(BF16)
-        live.update(g_one=g_one, g_three=g_three, sig=sig, grad_out=grad_out)
-
-    def grad_hidden(_):
-        loads[4].wait()
-        g_one, sig = live["g_one"], live["sig"]
-        d_hidden = mat(live["grad_out"], w_v[2], NT) * SCALE
-        dg_v[0] = (d_hidden * live["g_three"] * sig * (1.0 + g_one * (1.0 - sig))).astype(BF16)
-        dg_v[1] = (d_hidden * (g_one * sig)).astype(BF16)
+        if not own:
+            loads[7].wait()
+            loads[3].wait()
+            rate_col = jnp.broadcast_to(rate_v[...], (128, DH)).T
+            rate_wide = jnp.concatenate([rate_col] * 4, axis=1)
+            live["grad_out"] = (-(rate_wide * v_v[...].astype(F32))).astype(BF16)
+        loc[2, cols, :] = (mat(hidden, live["grad_out"], TN) * SCALE).astype(BF16)
+        live[own] = g_one, g_three, sig
+
+    def grad_hidden(own):
+        if not own:
+            loads[4].wait()
+        cols = columns(own)
+        g_one, g_three, sig = live[own]
+        d_hidden = mat(live["grad_out"], w_v[2, cols, :], NT) * SCALE
+        dg_v[0, :, cols] = (d_hidden * g_three * sig * (1.0 + g_one * (1.0 - sig))).astype(BF16)
+        dg_v[1, :, cols] = (d_hidden * (g_one * sig)).astype(BF16)
 
     def grad_one_three(mine):
         m = core if mine else 1 - core
@@ -278,12 +290,21 @@
             copy.wait_send()
 
 
+def closing_kernel(layer, weights, layer_out, new_weights, sems):
+    copies = [pltpu.make_async_copy(weights.at[0, m], new_weights.at[0, m], sems.at[m]) for m in range(3)]
+    copies.append(pltpu.make_async_copy(layer, layer_out, sems.at[3]))
+    for copy in copies:
+        copy.start()
+    for copy in copies:
+        copy.wait()
+
+
 def local(keys, values, rates, queries, fast_weights, gate, gain):
     operands = (keys, values, rates, queries, fast_weights, gate, gain.reshape(1, HEADS * DH))
     vmem = pl.BlockSpec(memory_space=pltpu.VMEM)
     hbm = pl.BlockSpec(memory_space=pltpu.HBM)
     dma = pltpu.SemaphoreType.DMA
-    return pl.pallas_call(
+    results = pl.pallas_call(
         functools.partial(memory_kernel, SCHEDULE),
         name="memory_layer",
         out_shape=(
@@ -323,6 +344,18 @@
             collective_id=0, has_side_effects=True, vmem_limit_bytes=44 * 2**20
         ),
     )(*(pltpu.with_memory_space_constraint(operand, pltpu.HBM) for operand in operands))
+    return pl.pallas_call(
+        closing_kernel,
+        name="closing_copy",
+        out_shape=(
+            jax.ShapeDtypeStruct((64, HEADS * DH), BF16),
+            jax.ShapeDtypeStruct((1, 3, DH, DH), BF16),
+        ),
+        in_specs=[vmem] * 2,
+        out_specs=(hbm, hbm),
+        scratch_shapes=[dma((4,))],
+        compiler_params=pltpu.CompilerParams(vmem_limit_bytes=16 * 2**20),
+    )(*(pltpu.with_memory_space_constraint(result, pltpu.VMEM) for result in results))
 
 
 def solution(mesh):

time: 53.5 us -> 53.2 us (level)
  local copies, waits for them, and re-layouts: 1.94 us -> 0 us
  Pallas kernels: 50.9 us -> 52.5 us
    unnamed x2 -> x0, local copies, waits for them, and re-layouts: 1.94 us -> none
    pallas_call x0 -> x1, Pallas kernels: none -> 1.35 us  [local(): pl.pallas_call(closing_kernel, name='closing_copy', out_shape=(jax.ShapeD...]
where the time goes in v5:
time: 53.2 us; the launch traced here: 53.1 us
  Pallas kernels  52.5 us (99%)
  between operations  0.64 us (1%)
    pallas_call x1, Pallas kernels, local(): pl.pallas_call(functools.partial(memory_kernel, SCHEDULE), name='memory_l...  51.1 us
    pallas_call x1, Pallas kernels, local(): pl.pallas_call(closing_kernel, name='closing_copy', out_shape=(jax.ShapeD...  1.35 us

profile of v5, /device:TPU:1, one launch (start us, length us, event | category | flops | bytes accessed | tf_op | source)
XLA Modules:
  0.0 53.1 jit_solution(15521194078715896975)
XLA Ops:
  0.6 51.1 %memory_layer.1 = (bf16[64,4096]{1,0:T(8,128)(2,1)S(1)}, bf16[1,3,512,512]{3,2,1,0:T(8,128)(2,1)S(1)}) custom-call(bf16[512,512]{1,0:T(8,128)(2,1)} %keys.1, bf16[512,512]{1,0:T(8,128)(2,1)} %values.1, f32[1,512]{1,0:T(1,128)} %rates.1, bf16[64,4096]{1,0:T(8,128)(2,1)} %queries.1, bf16[1,3,512,512]{3,2,1,0:T(8,128)(2,1)} %weights.1, bf16[64,4096]{1,0:T(8,128)(2,1)} %gate.1, ...), custom_call_target="tpu_custom_call" | custom-call | tf_op jit(solution)/shard_map/memory_layer/pallas_call | solution.py:307
  51.7 1.3 %closing_copy.1 = (bf16[64,4096]{1,0:T(8,128)(2,1)}, bf16[1,3,512,512]{3,2,1,0:T(8,128)(2,1)}) custom-call(bf16[64,4096]{1,0:T(8,128)(2,1)S(1)} %get-tuple-element.4.layer, bf16[1,3,512,512]{3,2,1,0:T(8,128)(2,1)S(1)} %get-tuple-element.5.weights), custom_call_target="tpu_custom_call" | custom-call | tf_op jit(solution)/shard_map/closing_copy/pallas_call | solution.py:347

commit v6 on v5

--- a/solution.py
+++ b/solution.py
@@ -26,16 +26,16 @@
 SCHEDULE = (
     ("grad_two", 0), ("greet", 0), ("core_send", 2), ("query_send", 0), ("grad_two", 1), ("x_send", 2),
     ("grad_hidden", 0), ("grad_hidden", 1), ("grad_one_three", 0), ("core_send", 0), ("core_send", 1),
-    ("grad_one_three", 1), ("x_send", 0), ("x_send", 1), ("z_send", 2), ("z_send", 0), ("z_send", 1), ("readout", 0),
-    ("y_send", 2), ("y_send", 0), ("y_send", 1), ("read_send", 0), ("a_send", 2), ("a_send", 0), ("a_send", 1),
+    ("grad_one_three", 1), ("x_send", 0), ("x_send", 1), ("z_send", 2), ("z_send", 0), ("z_send", 1), ("y_send", 2),
+    ("readout", 0), ("y_send", 0), ("y_send", 1), ("read_send", 0), ("a_send", 2), ("a_send", 0), ("a_send", 1),
     ("forward_two", 2), ("normalise", 0), ("orthogonal", 0), ("orthogonal", 0), ("orthogonal", 0), ("orthogonal", 0),
-    ("orthogonal", 0), ("orthogonal", 0), ("orthogonal", 0), ("orthogonal", 0), ("orthogonal", 0), ("orthogonal", 0),
-    ("orthogonal", 0), ("orthogonal", 0), ("orthogonal", 0), ("orthogonal", 0), ("orthogonal", 0), ("update", 0),
-    ("read_wait", 0), ("finish_read", 0), ("finish_read", 1), ("finish_read", 2), ("finish_read", 3),
-    ("finish_read", 4), ("finish_read", 5), ("finish_read", 6), ("finish_read", 7), ("normalise", 1),
-    ("orthogonal", 1), ("orthogonal", 1), ("orthogonal", 1), ("orthogonal", 1), ("orthogonal", 1), ("orthogonal", 1),
-    ("orthogonal", 1), ("orthogonal", 1), ("orthogonal", 1), ("orthogonal", 1), ("orthogonal", 1), ("orthogonal", 1),
-    ("orthogonal", 1), ("orthogonal", 1), ("update_own", 0), ("update_own", 1),
+    ("orthogonal", 0), ("orthogonal", 0), ("orthogonal", 0), ("orthogonal", 0), ("orthogonal", 0), ("normalise", 1),
+    ("orthogonal", 1), ("orthogonal", 0), ("orthogonal", 1), ("orthogonal", 0), ("orthogonal", 1), ("orthogonal", 0),
+    ("orthogonal", 1), ("orthogonal", 0), ("orthogonal", 1), ("orthogonal", 0), ("orthogonal", 1), ("orthogonal", 0),
+    ("orthogonal", 1), ("update", 0), ("orthogonal", 1), ("orthogonal", 1), ("orthogonal", 1), ("orthogonal", 1),
+    ("orthogonal", 1), ("orthogonal", 1), ("orthogonal", 1), ("update_own", 0), ("update_own", 1), ("read_wait", 0),
+    ("finish_read", 0), ("finish_read", 1), ("finish_read", 2), ("finish_read", 3), ("finish_read", 4),
+    ("finish_read", 5), ("finish_read", 6), ("finish_read", 7),
 )
 HALVES = (slice(0, 256), slice(256, 512))
 

time: 53.2 us -> 51.2 us (0.962)
  Pallas kernels: 52.5 us -> 50.5 us
    pallas_call x1, Pallas kernels: 51.1 us -> 49.1 us  [local(): pl.pallas_call(functools.partial(memory_kernel, SCHEDULE), name='memory_l...]
where the time goes in v6:
time: 51.2 us; the launch traced here: 51.1 us
  Pallas kernels  50.5 us (99%)
  between operations  0.64 us (1%)
    pallas_call x1, Pallas kernels, local(): pl.pallas_call(functools.partial(memory_kernel, SCHEDULE), name='memory_l...  49.1 us
    pallas_call x1, Pallas kernels, local(): pl.pallas_call(closing_kernel, name='closing_copy', out_shape=(jax.ShapeD...  1.35 us

profile of v6, /device:TPU:1, one launch (start us, length us, event | category | flops | bytes accessed | tf_op | source)
XLA Modules:
  0.0 51.1 jit_solution(10408947052755318786)
XLA Ops:
  0.6 49.1 %memory_layer.1 = (bf16[64,4096]{1,0:T(8,128)(2,1)S(1)}, bf16[1,3,512,512]{3,2,1,0:T(8,128)(2,1)S(1)}) custom-call(bf16[512,512]{1,0:T(8,128)(2,1)} %keys.1, bf16[512,512]{1,0:T(8,128)(2,1)} %values.1, f32[1,512]{1,0:T(1,128)} %rates.1, bf16[64,4096]{1,0:T(8,128)(2,1)} %queries.1, bf16[1,3,512,512]{3,2,1,0:T(8,128)(2,1)} %weights.1, bf16[64,4096]{1,0:T(8,128)(2,1)} %gate.1, ...), custom_call_target="tpu_custom_call" | custom-call | tf_op jit(solution)/shard_map/memory_layer/pallas_call | solution.py:307
  49.8 1.3 %closing_copy.1 = (bf16[64,4096]{1,0:T(8,128)(2,1)}, bf16[1,3,512,512]{3,2,1,0:T(8,128)(2,1)}) custom-call(bf16[64,4096]{1,0:T(8,128)(2,1)S(1)} %get-tuple-element.4.layer, bf16[1,3,512,512]{3,2,1,0:T(8,128)(2,1)S(1)} %get-tuple-element.5.weights), custom_call_target="tpu_custom_call" | custom-call | tf_op jit(solution)/shard_map/closing_copy/pallas_call | solution.py:347

commit v7 on v6

--- a/solution.py
+++ b/solution.py
@@ -178,7 +178,7 @@
         arrived(("c", m))
         mine = rows_of(m, core)[...].astype(F32)
         part[m] = (mine + c_recv[m].astype(F32)).astype(BF16).reshape(4, 64, DH)
-        for d in (1, 3, 2):
+        for d in (2, 1, 3):
             start(("x", m), remote(
                 part.at[m, x_other(d)], x_recv.at[m, d - 1], x_ss.at[m, d - 1], x_rs.at[m, d - 1],
                 at(x_other(d), zi, core),
@@ -190,7 +190,7 @@
         for d in range(3):
             total = total + x_recv[m, d].astype(F32)
         z_part[m] = total.astype(BF16).reshape(4, 16, DH)
-        for d in (1, 3, 2):
+        for d in (2, 1, 3):
             start(("z", m), remote(
                 z_part.at[m, z_other(d)], z_recv.at[m, d - 1], z_ss.at[m, d - 1], z_rs.at[m, d - 1],
                 at(xi, z_other(d), core),
@@ -203,19 +203,19 @@
             total = total + z_recv[m, d].astype(F32)
         block = block_of(m, xi, zi)
         block[...] = total.astype(BF16)
-        for d in (1, 3, 2):
+        for d in (2, 1, 3):
             start(("y", m), remote(block, block, y_ss.at[m, d - 1], y_rs.at[m, d - 1], at(xi, z_other(d), core)))
 
     def a_send(m):
         arrived(("y", m))
         block = block_of(m, xi)
-        for d in (1, 3, 2):
+        for d in (2, 1, 3):
             start(("a", m), remote(block, block, a_ss.at[m, d - 1], a_rs.at[m, d - 1], at(x_other(d), zi, core)))
         if m == 2:
             start(("f", m), remote(block, block, f_ss.at[0], f_rs.at[0], sibling))
 
     def forward_two(_):
-        for i, d in enumerate((1, 3, 2)):
+        for i, d in enumerate((2, 1, 3)):
             copies["a", 2][i].wait_recv()
             block = block_of(2, (xi + 4 - d) % 4)
             start(("f", 2), remote(block, block, f_ss.at[d], f_rs.at[d], sibling))

time: 51.2 us -> 50.5 us (0.986)
  Pallas kernels: 50.5 us -> 49.8 us
    pallas_call x1, Pallas kernels: 49.1 us -> 48.5 us  [local(): pl.pallas_call(functools.partial(memory_kernel, SCHEDULE), name='memory_l...]
where the time goes in v7:
time: 50.5 us
  Pallas kernels  49.8 us (99%)
  between operations  0.64 us (1%)
    pallas_call x1, Pallas kernels, local(): pl.pallas_call(functools.partial(memory_kernel, SCHEDULE), name='memory_l...  48.5 us
    pallas_call x1, Pallas kernels, local(): pl.pallas_call(closing_kernel, name='closing_copy', out_shape=(jax.ShapeD...  1.35 us

profile of v7, /device:TPU:1, one launch (start us, length us, event | category | flops | bytes accessed | tf_op | source)
XLA Modules:
  0.0 50.5 jit_solution(1807619303068426641)
XLA Ops:
  0.6 48.5 %memory_layer.1 = (bf16[64,4096]{1,0:T(8,128)(2,1)S(1)}, bf16[1,3,512,512]{3,2,1,0:T(8,128)(2,1)S(1)}) custom-call(bf16[512,512]{1,0:T(8,128)(2,1)} %keys.1, bf16[512,512]{1,0:T(8,128)(2,1)} %values.1, f32[1,512]{1,0:T(1,128)} %rates.1, bf16[64,4096]{1,0:T(8,128)(2,1)} %queries.1, bf16[1,3,512,512]{3,2,1,0:T(8,128)(2,1)} %weights.1, bf16[64,4096]{1,0:T(8,128)(2,1)} %gate.1, ...), custom_call_target="tpu_custom_call" | custom-call | tf_op jit(solution)/shard_map/memory_layer/pallas_call | solution.py:307
  49.1 1.3 %closing_copy.1 = (bf16[64,4096]{1,0:T(8,128)(2,1)}, bf16[1,3,512,512]{3,2,1,0:T(8,128)(2,1)}) custom-call(bf16[64,4096]{1,0:T(8,128)(2,1)S(1)} %get-tuple-element.4.layer, bf16[1,3,512,512]{3,2,1,0:T(8,128)(2,1)S(1)} %get-tuple-element.5.weights), custom_call_target="tpu_custom_call" | custom-call | tf_op jit(solution)/shard_map/closing_copy/pallas_call | solution.py:347

commit v8 on v7

--- a/solution.py
+++ b/solution.py
@@ -81,7 +81,7 @@
         return (zi + d) % 4
 
     sibling = at(xi, zi, 1 - core)
-    heads_other = [(head + d) % HEADS for d in range(1, HEADS)]
+    heads_other = [(head + d) % HEADS for d in (4, 5, 3, 2, 6, 1, 7)]
 
     def remote(src, dst, ss, rs, target):
         return pltpu.make_async_remote_copy(
@@ -232,10 +232,12 @@
 
     def update_own(half):
         cols = HALVES[half]
-        last = (COEF_A * x_it[1, :, cols].astype(F32) + mat(poly[1], x_it[1, :, cols])).astype(BF16)
-        new_weights[0, core, :, cols] = (w_v[core, :, cols].astype(F32) - STEP_SIZE * last.astype(F32)).astype(BF16)
-        block = new_weights.at[0, core, :, cols]
-        start("e", remote(block, block, e_ss.at[half], e_rs.at[half], sibling))
+        for i, rows in enumerate(HALVES):
+            last = COEF_A * x_it[1, rows, cols].astype(F32) + mat(poly[1, rows], x_it[1, :, cols])
+            last = last.astype(BF16).astype(F32)
+            new_weights[0, core, rows, cols] = (w_v[core, rows, cols].astype(F32) - STEP_SIZE * last).astype(BF16)
+            block = new_weights.at[0, core, rows, cols]
+            start("e", remote(block, block, e_ss.at[2 * half + i], e_rs.at[2 * half + i], sibling))
 
     def query_send(_):
         for d, h in enumerate(heads_other):
@@ -338,7 +340,7 @@
             dma((7,)), dma((7,)), dma((7,)), dma((7,)),
             dma((3,)), dma((3,)),
             dma((3, 3)), dma((3, 3)), dma((3, 3)), dma((3, 3)), dma((3, 3)), dma((3, 3)), dma((3, 3)), dma((3, 3)),
-            dma((4,)), dma((4,)), dma((2,)), dma((2,)),
+            dma((4,)), dma((4,)), dma((4,)), dma((4,)),
         ],
         compiler_params=pltpu.CompilerParams(
             collective_id=0, has_side_effects=True, vmem_limit_bytes=44 * 2**20

time: 50.5 us -> 50.5 us (level)
  no operation moved by 1% of the time
where the time goes in v8:
time: 50.5 us; the launch traced here: 50.4 us
  Pallas kernels  49.8 us (99%)
  between operations  0.64 us (1%)
    pallas_call x1, Pallas kernels, local(): pl.pallas_call(functools.partial(memory_kernel, SCHEDULE), name='memory_l...  48.4 us
    pallas_call x1, Pallas kernels, local(): pl.pallas_call(closing_kernel, name='closing_copy', out_shape=(jax.ShapeD...  1.35 us

profile of v8, /device:TPU:1, one launch (start us, length us, event | category | flops | bytes accessed | tf_op | source)
XLA Modules:
  0.0 50.4 jit_solution(2124212802354156675)
XLA Ops:
  0.6 48.4 %memory_layer.1 = (bf16[64,4096]{1,0:T(8,128)(2,1)S(1)}, bf16[1,3,512,512]{3,2,1,0:T(8,128)(2,1)S(1)}) custom-call(bf16[512,512]{1,0:T(8,128)(2,1)} %keys.1, bf16[512,512]{1,0:T(8,128)(2,1)} %values.1, f32[1,512]{1,0:T(1,128)} %rates.1, bf16[64,4096]{1,0:T(8,128)(2,1)} %queries.1, bf16[1,3,512,512]{3,2,1,0:T(8,128)(2,1)} %weights.1, bf16[64,4096]{1,0:T(8,128)(2,1)} %gate.1, ...), custom_call_target="tpu_custom_call" | custom-call | tf_op jit(solution)/shard_map/memory_layer/pallas_call | solution.py:309
  49.1 1.3 %closing_copy.1 = (bf16[64,4096]{1,0:T(8,128)(2,1)}, bf16[1,3,512,512]{3,2,1,0:T(8,128)(2,1)}) custom-call(bf16[64,4096]{1,0:T(8,128)(2,1)S(1)} %get-tuple-element.4.layer, bf16[1,3,512,512]{3,2,1,0:T(8,128)(2,1)S(1)} %get-tuple-element.5.weights), custom_call_target="tpu_custom_call" | custom-call | tf_op jit(solution)/shard_map/closing_copy/pallas_call | solution.py:349

commit v9 on v7

--- a/solution.py
+++ b/solution.py
@@ -221,11 +221,16 @@
             start(("f", 2), remote(block, block, f_ss.at[d], f_rs.at[d], sibling))
 
     def normalise(slot):
-        for key in (("f", 2),) if slot == 0 else (("a", 0), ("a", 1)):
-            arrived(key)
-        grad = full[slot].reshape(DH, DH).astype(F32)
-        norm = jnp.sqrt(jnp.sum(grad * grad)) + 1e-07
-        x_it[slot] = (grad / norm).astype(BF16)
+        keys_of = (("f", 2),) if slot == 0 else (("a", 0), ("a", 1))
+        total = 0.0
+        for i, rows in enumerate(HALVES):
+            if i < len(keys_of):
+                arrived(keys_of[i])
+            grad = full[slot, i].reshape(256, DH).astype(F32)
+            total = total + jnp.sum(grad * grad)
+        inverse = 1.0 / (jnp.sqrt(total) + 1e-07)
+        for i, rows in enumerate(HALVES):
+            x_it[slot, rows, :] = (full[slot, i].reshape(256, DH).astype(F32) * inverse).astype(BF16)
 
     def update(_):
         new_weights[0, 2] = (w_v[2].astype(F32) - STEP_SIZE * x_it[0].astype(F32)).astype(BF16)

time: 50.5 us -> 50.6 us (level)
  no operation moved by 1% of the time
where the time goes in v9:
time: 50.6 us; the launch traced here: 50.5 us
  Pallas kernels  49.9 us (99%)
  between operations  0.64 us (1%)
    pallas_call x1, Pallas kernels, local(): pl.pallas_call(functools.partial(memory_kernel, SCHEDULE), name='memory_l...  48.5 us
    pallas_call x1, Pallas kernels, local(): pl.pallas_call(closing_kernel, name='closing_copy', out_shape=(jax.ShapeD...  1.35 us

profile of v9, /device:TPU:1, one launch (start us, length us, event | category | flops | bytes accessed | tf_op | source)
XLA Modules:
  0.0 50.5 jit_solution(13689927506045627970)
XLA Ops:
  0.6 48.5 %memory_layer.1 = (bf16[64,4096]{1,0:T(8,128)(2,1)S(1)}, bf16[1,3,512,512]{3,2,1,0:T(8,128)(2,1)S(1)}) custom-call(bf16[512,512]{1,0:T(8,128)(2,1)} %keys.1, bf16[512,512]{1,0:T(8,128)(2,1)} %values.1, f32[1,512]{1,0:T(1,128)} %rates.1, bf16[64,4096]{1,0:T(8,128)(2,1)} %queries.1, bf16[1,3,512,512]{3,2,1,0:T(8,128)(2,1)} %weights.1, bf16[64,4096]{1,0:T(8,128)(2,1)} %gate.1, ...), custom_call_target="tpu_custom_call" | custom-call | tf_op jit(solution)/shard_map/memory_layer/pallas_call | solution.py:312
  49.2 1.3 %closing_copy.1 = (bf16[64,4096]{1,0:T(8,128)(2,1)}, bf16[1,3,512,512]{3,2,1,0:T(8,128)(2,1)}) custom-call(bf16[64,4096]{1,0:T(8,128)(2,1)S(1)} %get-tuple-element.4.layer, bf16[1,3,512,512]{3,2,1,0:T(8,128)(2,1)S(1)} %get-tuple-element.5.weights), custom_call_target="tpu_custom_call" | custom-call | tf_op jit(solution)/shard_map/closing_copy/pallas_call | solution.py:352
